TPU v7x, 32 devices: a whole 2x2x4 slice. The times are simulated.
32 devices in a mesh: seq: 8 (over z, x), rows: 4 (over y, core).
Axes of the slice: x: 2, y: 2, z: 4, core: 2. Of those that a mesh axis runs over, the one named last changes fastest.
Arguments:
- tokens: bfloat16 [2, 4, 1024, 2048], P(None, 'rows', 'seq'), may hold values from -6 to 6
- doc_lengths: int32 [2, 4, 8], P(None, 'rows'), may hold values from 1 to 1017, as said below
- ln1_gain: bfloat16 [2048], P(('seq', 'rows')), may hold values from 0.5 to 1.5
- ln1_bias: bfloat16 [2048], P(('seq', 'rows')), may hold values from -1.75 to 1.75
- w_qkv: bfloat16 [2048, 6144], P(('seq', 'rows')), may hold values from -0.125 to 0.125
- q_bias: bfloat16 [2048], P(('seq', 'rows')), may hold values from -3 to 3
- k_bias_rot: bfloat16 [512], P(('seq', 'rows')), may hold values from -6 to 6
- v_bias: bfloat16 [2048], P(('seq', 'rows')), may hold values from -3 to 3
- w_out: bfloat16 [2048, 2048], P(('seq', 'rows')), may hold values from -0.5 to 0.5
- ln2_gain: bfloat16 [2048], P(('seq', 'rows')), may hold values from 0.5 to 1.5
- ln2_bias: bfloat16 [2048], P(('seq', 'rows')), may hold values from -1.75 to 1.75
- w_gate: bfloat16 [2048, 5632], P(('seq', 'rows')), may hold values from -0.125 to 0.125
- w_up: bfloat16 [2048, 5632], P(('seq', 'rows')), may hold values from -0.125 to 0.125
- w_down: bfloat16 [5632, 2048], P(('seq', 'rows')), may hold values from -0.078125 to 0.078125
- cotangent: bfloat16 [2, 4, 1024, 2048], P(None, 'rows', 'seq'), may hold values from -6 to 6
Outputs:
- output: bfloat16 [2, 4, 1024, 2048], P(None, 'rows', 'seq')
- grad_tokens: bfloat16 [2, 4, 1024, 2048], P(None, 'rows', 'seq')
- grad_ln1_gain: float32 [2048], P(('seq', 'rows'))
- grad_ln1_bias: float32 [2048], P(('seq', 'rows'))
- grad_w_qkv: float32 [2048, 6144], P(('seq', 'rows'))
- grad_q_bias: float32 [2048], P(('seq', 'rows'))
- grad_k_bias_rot: float32 [512], P(('seq', 'rows'))
- grad_v_bias: float32 [2048], P(('seq', 'rows'))
- grad_w_out: float32 [2048, 2048], P(('seq', 'rows'))
- grad_ln2_gain: float32 [2048], P(('seq', 'rows'))
- grad_ln2_bias: float32 [2048], P(('seq', 'rows'))
- grad_w_gate: float32 [2048, 5632], P(('seq', 'rows'))
- grad_w_up: float32 [2048, 5632], P(('seq', 'rows'))
- grad_w_down: float32 [5632, 2048], P(('seq', 'rows'))
Inputs may be any that keep to these rules, and one draw needn't show every extreme that they name: `doc_lengths`: the 8 lengths of a row sum to 1024. A row holds either one document of 1017 tokens beside documents of one token, or two documents of about half the row beside short ones of at most 16 tokens; every index of rows has at least one row of the first kind among its micro-batches.
All inputs are finite; a program needn't handle non-finite values.
Results may differ from a plain program's by a relative error of at most 0.023.
Values may be sent and summed in bfloat16 or wider, within the bound.
A program may use at most 576 MiB of HBM per device.

v0:
```python
import jax
import jax.numpy as jnp
from jax import lax
from jax.sharding import PartitionSpec as P

D = 2048
HEADS = 32
HD = 64
ROT = 16
FF = 5632
MB = 2


NORM_EPS = 1e-05
THETA = 10000.0
MASKED = -1e30


def dot_last(left, right):
    return lax.dot_general(
        left, right, (((1,), (1,)), ((), ())), preferred_element_type=jnp.float32
    )


def dot_first(left, right):
    return lax.dot_general(
        left, right, (((0,), (0,)), ((), ())), preferred_element_type=jnp.float32
    )


def row_layout(lengths, row_len):
    doc_ends = jnp.cumsum(lengths, dtype=jnp.int32)
    places = jnp.arange(row_len, dtype=jnp.int32)
    passed = (places[:, None] >= doc_ends[None, :]).astype(jnp.int32)
    segment = jnp.sum(passed, axis=1, dtype=jnp.int32)
    starts = jnp.sum(passed * lengths[None, :], axis=1, dtype=jnp.int32)
    return (segment, places - starts)


def norm_forward(values, norm_gain, norm_bias):
    average = jnp.mean(values, axis=-1, keepdims=True)
    centred = values - average
    inv_dev = lax.rsqrt(jnp.mean(centred * centred, axis=-1, keepdims=True) + NORM_EPS)
    scaled = centred * inv_dev
    return (scaled * norm_gain + norm_bias, scaled, inv_dev)


def norm_backward(grad_normed, scaled, inv_dev, norm_gain):
    grad_scaled = grad_normed * norm_gain
    first_mean = jnp.mean(grad_scaled, axis=-1, keepdims=True)
    second_mean = jnp.mean(grad_scaled * scaled, axis=-1, keepdims=True)
    return inv_dev * (grad_scaled - first_mean - scaled * second_mean)


def rotary_tables(positions):
    half_rot = ROT // 2
    frequency = THETA ** (-2.0 * jnp.arange(half_rot, dtype=jnp.float32) / ROT)
    angles = positions.astype(jnp.float32)[:, None] * frequency[None, :]
    return (jnp.cos(angles)[:, None, :], jnp.sin(angles)[:, None, :])


def rotate(head_vals, cosine, sine_tab, orient):
    half_rot = ROT // 2
    low_half = head_vals[..., :half_rot]
    high_half = head_vals[..., half_rot:ROT]
    return jnp.concatenate(
        [
            low_half * cosine - orient * high_half * sine_tab,
            high_half * cosine + orient * low_half * sine_tab,
            head_vals[..., ROT:],
        ],
        axis=-1,
    )


def block_scores(query_blk, keys_all, segment, first_row, block_rows):
    places = jnp.arange(segment.shape[0], dtype=jnp.int32)
    query_places = first_row + jnp.arange(block_rows, dtype=jnp.int32)
    query_segs = lax.dynamic_slice_in_dim(segment, first_row, block_rows)
    allowed = (query_segs[:, None] == segment[None, :]) & (query_places[:, None] >= places[None, :])
    scores = jnp.einsum(
        "qhd,khd->hqk", query_blk, keys_all, preferred_element_type=jnp.float32
    ) * HD ** (-0.5)
    return jnp.where(allowed[None], scores, MASKED)


def attend_forward(head_view, segment, block_rows):
    row_len = head_view.shape[0]
    queries = head_view[:, 0].reshape(row_len, -1, HD)
    keys_all = head_view[:, 1].reshape(row_len, -1, HD)
    values_all = head_view[:, 2].reshape(row_len, -1, HD)

    def one_block(block_index):
        first_row = block_index * block_rows
        query_blk = lax.dynamic_slice_in_dim(queries, first_row, block_rows, 0)
        scores = block_scores(query_blk, keys_all, segment, first_row, block_rows)
        row_peak = jnp.max(scores, axis=-1, keepdims=True)
        raised = jnp.exp(scores - row_peak)
        totals = jnp.sum(raised, axis=-1, keepdims=True)
        probs_low = (raised / totals).astype(jnp.bfloat16)
        attended = jnp.einsum(
            "hqk,khd->qhd", probs_low, values_all, preferred_element_type=jnp.float32
        )
        return (
            attended.astype(jnp.bfloat16).reshape(block_rows, -1),
            (row_peak + jnp.log(totals))[..., 0],
        )

    attended, log_totals = lax.map(one_block, jnp.arange(row_len // block_rows, dtype=jnp.int32))
    return (attended.reshape(row_len, -1), log_totals)


def attend_backward(head_view, grad_heads, log_totals, segment, block_rows):
    row_len = head_view.shape[0]
    queries = head_view[:, 0].reshape(row_len, -1, HD)
    keys_all = head_view[:, 1].reshape(row_len, -1, HD)
    values_all = head_view[:, 2].reshape(row_len, -1, HD)
    grad_all = grad_heads.reshape(row_len, -1, HD)
    zeros_kv = jnp.zeros(keys_all.shape, jnp.float32)
    score_scale = HD ** (-0.5)

    def one_block(carry, block_data):
        grad_keys, grad_values = carry
        block_index, block_totals = block_data
        first_row = block_index * block_rows
        query_blk = lax.dynamic_slice_in_dim(queries, first_row, block_rows, 0)
        grad_blk = lax.dynamic_slice_in_dim(grad_all, first_row, block_rows, 0)
        scores = block_scores(query_blk, keys_all, segment, first_row, block_rows)
        attn_probs = jnp.exp(scores - block_totals[..., None])
        grad_probs = jnp.einsum(
            "qhd,khd->hqk", grad_blk, values_all, preferred_element_type=jnp.float32
        )
        inner_sum = jnp.sum(attn_probs * grad_probs, axis=-1, keepdims=True)
        grad_scores = (attn_probs * (grad_probs - inner_sum)).astype(jnp.bfloat16)
        grad_query = (
            jnp.einsum("hqk,khd->qhd", grad_scores, keys_all, preferred_element_type=jnp.float32)
            * score_scale
        )
        grad_keys = (
            grad_keys
            + jnp.einsum("hqk,qhd->khd", grad_scores, query_blk, preferred_element_type=jnp.float32)
            * score_scale
        )
        grad_values = grad_values + jnp.einsum(
            "hqk,qhd->khd",
            attn_probs.astype(jnp.bfloat16),
            grad_blk,
            preferred_element_type=jnp.float32,
        )
        return ((grad_keys, grad_values), grad_query.astype(jnp.bfloat16).reshape(block_rows, -1))

    block_ids = jnp.arange(row_len // block_rows, dtype=jnp.int32)
    (grad_keys, grad_values), grad_query = lax.scan(
        one_block, (zeros_kv, zeros_kv), (block_ids, log_totals)
    )
    return jnp.stack(
        [
            grad_query.reshape(row_len, -1),
            grad_keys.astype(jnp.bfloat16).reshape(row_len, -1),
            grad_values.astype(jnp.bfloat16).reshape(row_len, -1),
        ],
        axis=1,
    )


def make_terms(normed_one, attended, normed_two, grad_mixed, grad_branch, grad_gate, grad_up):

    def weight_terms(first_row, row_count):
        return jnp.concatenate(
            [
                dot_first(normed_one, grad_mixed),
                dot_first(attended, grad_branch),
                dot_first(normed_two, grad_gate),
                dot_first(normed_two, grad_up),
            ],
            axis=1,
        )

    return weight_terms


def local(
    tokens,
    doc_lengths,
    ln1_gain,
    ln1_bias,
    w_qkv,
    q_bias,
    k_bias_rot,
    v_bias,
    w_out,
    ln2_gain,
    ln2_bias,
    w_gate,
    w_up,
    w_down,
    cotangent,
):
    seq_count = lax.axis_size("seq")
    all_count = lax.axis_size(("seq", "rows"))
    local_len = tokens.shape[2]
    row_len = local_len * seq_count
    block_rows = min(512, row_len)
    local_first = lax.axis_index("seq") * local_len
    vector_zero = jnp.zeros((D // all_count,), jnp.float32)
    rot_share = jnp.zeros((HEADS * ROT // all_count,), jnp.float32)
    small_shares = [
        vector_zero,
        vector_zero,
        vector_zero,
        rot_share,
        vector_zero,
        vector_zero,
        vector_zero,
    ]
    full_zero = jnp.zeros((D,), jnp.float32)
    local_small = [
        full_zero,
        full_zero,
        full_zero,
        jnp.zeros((HEADS * ROT,), jnp.float32),
        full_zero,
        full_zero,
        full_zero,
    ]
    kept_acts = []
    outputs = []
    grads_in = []
    for micro_index in range(MB):
        gathered = (
            lax.all_gather(ln1_gain, ("seq", "rows"), axis=0, tiled=True),
            lax.all_gather(ln1_bias, ("seq", "rows"), axis=0, tiled=True),
            lax.all_gather(w_qkv, ("seq", "rows"), axis=0, tiled=True),
            lax.all_gather(q_bias, ("seq", "rows"), axis=0, tiled=True),
            lax.all_gather(k_bias_rot, ("seq", "rows"), axis=0, tiled=True),
            lax.all_gather(v_bias, ("seq", "rows"), axis=0, tiled=True),
            lax.all_gather(w_out, ("seq", "rows"), axis=0, tiled=True),
            lax.all_gather(ln2_gain, ("seq", "rows"), axis=0, tiled=True),
            lax.all_gather(ln2_bias, ("seq", "rows"), axis=0, tiled=True),
            lax.all_gather(w_gate, ("seq", "rows"), axis=0, tiled=True),
            lax.all_gather(w_up, ("seq", "rows"), axis=0, tiled=True),
            lax.all_gather(w_down, ("seq", "rows"), axis=0, tiled=True),
        )
        norm1_gain = gathered[0].astype(jnp.float32)
        norm1_bias = gathered[1].astype(jnp.float32)
        norm2_gain = gathered[7].astype(jnp.float32)
        norm2_bias = gathered[8].astype(jnp.float32)
        key_bias = jnp.concatenate(
            [
                gathered[4].astype(jnp.float32).reshape(HEADS, ROT),
                jnp.zeros((HEADS, HD - ROT), jnp.float32),
            ],
            axis=1,
        ).reshape(D)
        bias_all = jnp.concatenate(
            [gathered[3].astype(jnp.float32), key_bias, gathered[5].astype(jnp.float32)]
        )
        row_in = tokens[micro_index, 0].astype(jnp.float32)
        segment, positions = row_layout(doc_lengths[micro_index, 0], row_len)
        cosine, sine_tab = rotary_tables(
            lax.dynamic_slice_in_dim(positions, local_first, local_len)
        )
        normed_one, scaled_one, inv_one = norm_forward(row_in, norm1_gain, norm1_bias)
        normed_one = normed_one.astype(jnp.bfloat16)
        mixed = jnp.dot(normed_one, gathered[2], preferred_element_type=jnp.float32) + bias_all
        query_loc = rotate(
            mixed[:, :D].reshape(local_len, HEADS, HD), cosine, sine_tab, 1.0
        ).reshape(local_len, D)
        key_loc = rotate(
            mixed[:, D : 2 * D].reshape(local_len, HEADS, HD), cosine, sine_tab, 1.0
        ).reshape(local_len, D)
        stacked = jnp.stack([query_loc, key_loc, mixed[:, 2 * D :]], axis=1).astype(jnp.bfloat16)
        head_view = lax.all_to_all(stacked, "seq", split_axis=2, concat_axis=0, tiled=True)
        attended_heads, log_totals = attend_forward(head_view, segment, block_rows)
        attended = lax.all_to_all(attended_heads, "seq", split_axis=0, concat_axis=1, tiled=True)
        residual = row_in + jnp.dot(attended, gathered[6], preferred_element_type=jnp.float32)
        normed_two, scaled_two, inv_two = norm_forward(residual, norm2_gain, norm2_bias)
        normed_two = normed_two.astype(jnp.bfloat16)
        gate = jnp.dot(normed_two, gathered[9], preferred_element_type=jnp.float32)
        up_proj = jnp.dot(normed_two, gathered[10], preferred_element_type=jnp.float32)
        sigmoid_gate = jax.nn.sigmoid(gate)
        silu_gate = gate * sigmoid_gate
        hidden = (silu_gate * up_proj).astype(jnp.bfloat16)
        outputs.append(
            (residual + jnp.dot(hidden, gathered[11], preferred_element_type=jnp.float32)).astype(
                jnp.bfloat16
            )
        )
        grad_out = cotangent[micro_index, 0]
        grad_hidden = dot_last(grad_out, gathered[11])
        grad_gate = (
            grad_hidden * up_proj * sigmoid_gate * (1.0 + gate * (1.0 - sigmoid_gate))
        ).astype(jnp.bfloat16)
        grad_up = (grad_hidden * silu_gate).astype(jnp.bfloat16)
        grad_norm_two = dot_last(grad_gate, gathered[9]) + dot_last(grad_up, gathered[10])
        grad_residual = grad_out.astype(jnp.float32) + norm_backward(
            grad_norm_two, scaled_two, inv_two, norm2_gain
        )
        grad_branch = grad_residual.astype(jnp.bfloat16)
        grad_attended = dot_last(grad_branch, gathered[6]).astype(jnp.bfloat16)
        grad_heads = lax.all_to_all(grad_attended, "seq", split_axis=1, concat_axis=0, tiled=True)
        grad_view = attend_backward(head_view, grad_heads, log_totals, segment, block_rows)
        grad_local = lax.all_to_all(
            grad_view, "seq", split_axis=0, concat_axis=2, tiled=True
        ).astype(jnp.float32)
        grad_query = rotate(
            grad_local[:, 0].reshape(local_len, HEADS, HD), cosine, sine_tab, -1.0
        ).reshape(local_len, D)
        grad_key = rotate(
            grad_local[:, 1].reshape(local_len, HEADS, HD), cosine, sine_tab, -1.0
        ).reshape(local_len, D)
        grad_mixed = jnp.concatenate([grad_query, grad_key, grad_local[:, 2]], axis=1).astype(
            jnp.bfloat16
        )
        grad_norm_one = dot_last(grad_mixed, gathered[2])
        grads_in.append(
            (grad_residual + norm_backward(grad_norm_one, scaled_one, inv_one, norm1_gain)).astype(
                jnp.bfloat16
            )
        )
        mixed_sums = jnp.sum(grad_mixed.astype(jnp.float32), axis=0)
        key_sums = mixed_sums[D : 2 * D].reshape(HEADS, HD)[:, :ROT].reshape(HEADS * ROT)
        small_terms = [
            jnp.sum(grad_norm_one * scaled_one, axis=0),
            jnp.sum(grad_norm_one, axis=0),
            mixed_sums[:D],
            key_sums,
            mixed_sums[2 * D :],
            jnp.sum(grad_norm_two * scaled_two, axis=0),
            jnp.sum(grad_norm_two, axis=0),
        ]
        kept_acts.append(
            (
                normed_one,
                attended,
                normed_two,
                grad_mixed,
                grad_branch,
                grad_gate,
                grad_up,
                hidden,
                grad_out,
            )
        )
        local_small = [local_small[place] + small_terms[place] for place in range(7)]
    joined = [jnp.concatenate([kept[place] for kept in kept_acts], axis=0) for place in range(9)]
    weight_terms = make_terms(
        joined[0], joined[1], joined[2], joined[3], joined[4], joined[5], joined[6]
    )
    input_share = lax.psum_scatter(
        weight_terms(jnp.int32(0), D // all_count * lax.axis_size(("seq", "rows"))),
        ("seq", "rows"),
        scatter_dimension=0,
        tiled=True,
    )
    summed_rest = (
        lax.psum_scatter(
            dot_first(joined[7], joined[8]), ("seq", "rows"), scatter_dimension=0, tiled=True
        ),
        lax.psum_scatter(local_small[0], ("seq", "rows"), scatter_dimension=0, tiled=True),
        lax.psum_scatter(local_small[1], ("seq", "rows"), scatter_dimension=0, tiled=True),
        lax.psum_scatter(local_small[2], ("seq", "rows"), scatter_dimension=0, tiled=True),
        lax.psum_scatter(local_small[3], ("seq", "rows"), scatter_dimension=0, tiled=True),
        lax.psum_scatter(local_small[4], ("seq", "rows"), scatter_dimension=0, tiled=True),
        lax.psum_scatter(local_small[5], ("seq", "rows"), scatter_dimension=0, tiled=True),
        lax.psum_scatter(local_small[6], ("seq", "rows"), scatter_dimension=0, tiled=True),
    )
    down_share = summed_rest[0]
    small_shares = [summed_rest[place + 1] for place in range(7)]
    output = jnp.stack(outputs)[:, None]
    grad_tokens = jnp.stack(grads_in)[:, None]
    return (
        output,
        grad_tokens,
        small_shares[0],
        small_shares[1],
        input_share[:, : 3 * D],
        small_shares[2],
        small_shares[3],
        small_shares[4],
        input_share[:, 3 * D : 4 * D],
        small_shares[5],
        small_shares[6],
        input_share[:, 4 * D : 4 * D + FF],
        input_share[:, 4 * D + FF :],
        down_share,
    )


def solution(mesh):
    return jax.shard_map(
        local,
        mesh=mesh,
        in_specs=(
            P(None, "rows", "seq", None),
            P(None, "rows", None),
            P(("seq", "rows")),
            P(("seq", "rows")),
            P(("seq", "rows"), None),
            P(("seq", "rows")),
            P(("seq", "rows")),
            P(("seq", "rows")),
            P(("seq", "rows"), None),
            P(("seq", "rows")),
            P(("seq", "rows")),
            P(("seq", "rows"), None),
            P(("seq", "rows"), None),
            P(("seq", "rows"), None),
            P(None, "rows", "seq", None),
        ),
        out_specs=(
            P(None, "rows", "seq", None),
            P(None, "rows", "seq", None),
            P(("seq", "rows")),
            P(("seq", "rows")),
            P(("seq", "rows"), None),
            P(("seq", "rows")),
            P(("seq", "rows")),
            P(("seq", "rows")),
            P(("seq", "rows"), None),
            P(("seq", "rows")),
            P(("seq", "rows")),
            P(("seq", "rows"), None),
            P(("seq", "rows"), None),
            P(("seq", "rows"), None),
        ),
        check_vma=False,
    )
```

profile of v0, /device:TPU:1, one launch (start us, length us, event | category | flops | bytes accessed | tf_op | source)
XLA Modules:
  0.0 3366.8 jit_solution(4180789815812989719)
XLA Ops:
  12.8 43.4 %all-reduce.16 = (bf16[2048]{0:T(1024)(128)(2,1)S(1)}, bf16[2048]{0:T(1024)(128)(2,1)S(1)}, bf16[2048]{0:T(1024)(128)(2,1)S(1)}, bf16[512]{0:T(512)(128)(2,1)S(1...) all-reduce(bf16[2048]{0:T(1024)(128)(2,1)S(1)} %dynamic-update-slic, ...), channel_id=1, replica_groups=mesh['seq'=8,'rows'=4] {'seq','rows'}, use_global_device_ids=true, to_apply=%add.2 | all-reduce | flops 12800 | bytes 51200
  59.6 110.3 %all-gather.6.cloned.1.call-done = bf16[2048,6144]{1,0:T(8,128)(2,1)} async-done(((bf16[64,6144]{1,0:T(8,128)(2,1)}), bf16[2048,6144]{1,0:T(8,128)(2,1)}) %all-gather.6.cloned.1.call-update) | async-done | bytes 25165840 | tf_op jit(solution)/shard_map/all_gather | solution.py:233
  241.2 40.1 %all-to-all-done = bf16[128,3,2048]{0,1,2:T(4,128)(2,1)} async-done(((bf16[128,3,2048]{0,1,2:T(4,128)(2,1)}), bf16[128,3,2048]{0,1,2:T(4,128)(2,1)}, u32[]{:S(2)}, u32[]{:S(2)}) %all-to-all-start) | async-done | bytes 1572896 | tf_op jit(solution)/shard_map/all_to_all | solution.py:273
  289.8 19.6 while.54
  309.4 41.5 %all-to-all-done.2 = bf16[128,3,2048]{0,1,2:T(4,128)(2,1)} async-done(((bf16[128,3,2048]{0,1,2:T(4,128)(2,1)}), bf16[128,3,2048]{0,1,2:T(4,128)(2,1)}, u32[]{:S(2)}, u32[]{:S(2)}) %all-to-all-start.2) | async-done | bytes 1572896 | tf_op jit(solution)/shard_map/all_to_all | solution.py:273
  368.0 22.1 while.55
  398.0 25.3 all-to-all-done.3
  434.0 42.3 %all-gather.12.cloned.1.call-done = bf16[2048,5632]{1,0:T(8,128)(2,1)} async-done(((bf16[64,5632]{1,0:T(8,128)(2,1)}), bf16[2048,5632]{1,0:T(8,128)(2,1)}) %all-gather.12.cloned.1.call-update) | async-done | bytes 23068688 | tf_op jit(solution)/shard_map/all_gather | solution.py:241
  476.3 12.3 fusion.174
  488.5 133.1 %all-gather.10.cloned.1.call-done = bf16[2048,5632]{1,0:T(8,128)(2,1)} async-done(((bf16[64,5632]{1,0:T(8,128)(2,1)}), bf16[2048,5632]{1,0:T(8,128)(2,1)}) %all-gather.10.cloned.1.call-update) | async-done | bytes 23068688 | tf_op jit(solution)/shard_map/all_gather | solution.py:240
  621.7 12.5 fusion.173
  634.2 13.0 fusion.176
  653.1 114.1 %all-gather.14.cloned.1.call-done = bf16[5632,2048]{1,0:T(8,128)(2,1)} async-done(((bf16[176,2048]{1,0:T(8,128)(2,1)}), bf16[5632,2048]{1,0:T(8,128)(2,1)}) %all-gather.14.cloned.1.call-update) | async-done | bytes 23068688 | tf_op jit(solution)/shard_map/all_gather | solution.py:242
  767.2 15.3 multiply_convert_fusion.4
  782.5 13.3 fusion.177
  795.8 15.7 multiply_convert_fusion.2
  811.5 12.3 fusion.178
  823.8 11.9 convolution_add_fusion.2
  835.7 14.2 multiply_reduce_fusion.3
  884.0 19.6 fusion.88
  922.7 37.2 %while.57 = (s32[]{:T(128)}, f32[1024,4,64]{0,2,1:T(8,128)S(1)}, f32[1024,4,64]{0,2,1:T(8,128)}, bf16[2,512,256]{2,1,0:T(8,128)(2,1)}, s32[2]{0:T(128)S(1)}, /*i...) while((s32[]{:T(128)}, f32[1024,4,64]{0,2,1:T(8,128)S(1)}, ...), condition=%wide.region_33.34_spmd.clone, body=%wide.region_31.33_spmd.clone.sunk | while | flops 1376778752 | bytes 83695952 | solution.py:153
  970.9 34.0 %while.56 = (s32[]{:T(128)}, f32[1024,4,64]{0,2,1:T(8,128)S(1)}, f32[1024,4,64]{0,2,1:T(8,128)}, bf16[2,512,256]{2,1,0:T(8,128)(2,1)}, s32[2]{0:T(128)S(1)}, /*i...) while((s32[]{:T(128)}, f32[1024,4,64]{0,2,1:T(8,128)S(1)}, ...), condition=%wide.region_26.27_spmd.clone, body=%wide.region_24.26_spmd.clone.sunk | while | flops 1376778752 | bytes 81598768 | solution.py:153
  1022.4 19.1 fusion.84
  1048.2 21.1 all-to-all-done.5
  1078.9 19.8 fusion.72
  1098.7 102.9 %pad_maximum_fusion = f32[2048,19456]{1,0:T(8,128)} fusion(f32[2048,5632]{1,0:T(8,128)} %fusion.88, f32[2048,5632]{1,0:T(8,128)} %fusion.84, f32[2048,2048]{1,0:T(8,128)} %fusion.137, f32[2048,6144]{1,0:T(8,128)} %fusion.72), kind=kLoop, calls=%fused_computation.94 | loop fusion | flops 119537664 | bytes 318767104 | tf_op jit(solution)/shard_map/concatenate | solution.py:169
  1203.3 20.2 fusion.92
  1249.7 14.7 fusion.147
  1264.4 14.5 fusion.132
  1278.9 48.7 %all-reduce.15 = (f32[2048]{0:T(1024)S(1)}, f32[2048]{0:T(1024)S(1)}, f32[2048]{0:T(1024)S(1)}, f32[512]{0:T(512)S(1)}, f32[2048]{0:T(1024)S(1)}, /*index=5*/f32[2048]{0:T(1024)S(1)}, f32[2048]{0:T(1024)S(1)}) all-reduce(f32[2048]{0:T(1024)S(1)} %add.336, ...), channel_id=2, replica_groups=mesh['seq'=8,'rows'=4] {'seq','rows'}, use_global_device_ids=true, to_apply=%region_38.39.clone | all-reduce | flops 12800 | bytes 102400
  1335.9 1532.2 %reduce-scatter.3.cloned.1.call-done = f32[64,19456]{1,0:T(8,128)} async-done(((f32[2048,19456]{1,0:T(8,128)}), f32[64,19456]{1,0:T(8,128)}) %reduce-scatter.3.cloned.1.call-update) | async-done | bytes 4980752 | tf_op jit(solution)/shard_map/reduce_scatter | solution.py:350
  2876.1 483.4 %reduce-scatter.5.cloned.1.call-done = f32[176,2048]{1,0:T(8,128)} async-done(((f32[5632,2048]{1,0:T(8,128)}), f32[176,2048]{1,0:T(8,128)}) %reduce-scatter.5.cloned.1.call-update) | async-done | bytes 1441808 | tf_op jit(solution)/shard_map/reduce_scatter | solution.py:357
  (509 shorter events, 378.1 us)
Async XLA Ops:
  7.3 49.4 %copy-start.14 = (bf16[2,1,128,2048]{3,2,1,0:T(8,128)(2,1)S(1)}, bf16[2,1,128,2048]{3,2,1,0:T(8,128)(2,1)}, u32[]{:S(2)}) copy-start(bf16[2,1,128,2048]{3,2,1,0:T(8,128)(2,1)} %param.23) | copy-start | bytes 3145732
  7.3 162.6 %all-gather.6.cloned.1.call-start = ((), (), s32[]{:S(2)}) async-start(), calls=%async_computation.10 | async-start | bytes 25952256 | tf_op jit(solution)/shard_map/all_gather | solution.py:233
  8.0 416.3 %all-gather.8.cloned.1.call-start = ((), (), s32[]{:S(2)}) async-start(), calls=%async_computation.11 | async-start | bytes 8650752 | tf_op jit(solution)/shard_map/all_gather | solution.py:237
  8.8 467.5 %all-gather.12.cloned.1.call-start = ((), (), s32[]{:S(2)}) async-start(), calls=%async_computation.13 | async-start | bytes 23789568 | tf_op jit(solution)/shard_map/all_gather | solution.py:241
  9.5 612.2 %all-gather.10.cloned.1.call-start = ((), (), s32[]{:S(2)}) async-start(), calls=%async_computation.12 | async-start | bytes 23789568 | tf_op jit(solution)/shard_map/all_gather | solution.py:240
  10.1 757.1 %all-gather.14.cloned.1.call-start = ((), (), s32[]{:S(2)}) async-start(), calls=%async_computation.14 | async-start | bytes 23789568 | tf_op jit(solution)/shard_map/all_gather | solution.py:242
  56.2 123.8 %copy-start.63 = (f32[2048]{0:T(1024)}, f32[2048]{0:T(1024)S(1)}, u32[]{:S(2)}) copy-start(f32[2048]{0:T(1024)S(1)} %convert_element_type.197) | copy-start | bytes 24580
  56.7 123.3 %copy-start.59 = (f32[6144]{0:T(1024)}, f32[6144]{0:T(1024)S(1)}, u32[]{:S(2)}) copy-start(f32[6144]{0:T(1024)S(1)} %maximum_convert_fusion) | copy-start | bytes 73732
  56.9 123.1 %copy-start.76 = (f32[128]{0:T(128)}, f32[128]{0:T(128)S(1)}, u32[]{:S(2)}) copy-start(f32[128]{0:T(128)S(1)} %get-tuple-element.657) | copy-start | bytes 1540
  56.9 123.1 %copy-start.78 = (f32[128]{0:T(128)}, f32[128]{0:T(128)S(1)}, u32[]{:S(2)}) copy-start(f32[128]{0:T(128)S(1)} %get-tuple-element.658) | copy-start | bytes 1540
  57.4 122.7 %copy-start.82 = (f32[128]{0:T(128)}, f32[128]{0:T(128)S(1)}, u32[]{:S(2)}) copy-start(f32[128]{0:T(128)S(1)} %add_rsqrt_fusion.3) | copy-start | bytes 1540
  57.4 122.7 %copy-start.84 = (f32[128]{0:T(128)}, f32[128]{0:T(128)S(1)}, u32[]{:S(2)}) copy-start(f32[128]{0:T(128)S(1)} %add_rsqrt_fusion.1) | copy-start | bytes 1540
  58.1 131.6 %copy-start.67 = (f32[128,8]{0,1:T(8,128)}, f32[128,8]{0,1:T(8,128)S(1)}, u32[]{:S(2)}) copy-start(f32[128,8]{0,1:T(8,128)S(1)} %get-tuple-element.638) | copy-start | bytes 12292
  58.1 169.5 %copy-start.65 = (f32[128,8]{0,1:T(8,128)}, f32[128,8]{0,1:T(8,128)S(1)}, u32[]{:S(2)}) copy-start(f32[128,8]{0,1:T(8,128)S(1)} %get-tuple-element.647) | copy-start | bytes 12292
  203.3 78.0 %all-to-all-start = ((bf16[128,3,2048]{0,1,2:T(4,128)(2,1)}), bf16[128,3,2048]{0,1,2:T(4,128)(2,1)}, u32[]{:S(2)}, u32[]{:S(2)}) async-start(bf16[128,3,2048]{0,1,2:T(4,128)(2,1)} %copy.190), calls=%async_computation | async-start | bytes 4194304 | tf_op jit(solution)/shard_map/all_to_all | solution.py:273
  281.3 69.6 %all-to-all-start.2 = ((bf16[128,3,2048]{0,1,2:T(4,128)(2,1)}), bf16[128,3,2048]{0,1,2:T(4,128)(2,1)}, u32[]{:S(2)}, u32[]{:S(2)}) async-start(bf16[128,3,2048]{0,1,2:T(4,128)(2,1)} %copy.202), calls=%async_computation.2 | async-start | bytes 4194304 | tf_op jit(solution)/shard_map/all_to_all | solution.py:273
  309.3 53.9 %copy-start.61 = (f32[2,4,512]{2,1,0:T(4,128)}, f32[2,4,512]{2,1,0:T(4,128)S(1)}, u32[]{:S(2)}) copy-start(f32[2,4,512]{2,1,0:T(4,128)S(1)} %get-tuple-element.1032) | copy-start | bytes 49156
  309.3 55.7 %copy-start.1 = (bf16[1024,4,64]{0,2,1:T(8,128)(2,1)}, bf16[1024,4,64]{0,2,1:T(8,128)(2,1)S(1)}, u32[]{:S(2)}) copy-start(bf16[1024,4,64]{0,2,1:T(8,128)(2,1)S(1)} %get-tuple-element.1082) | copy-start | bytes 1572868
  309.3 55.7 %copy-start.5 = (bf16[1024,4,64]{0,2,1:T(8,128)(2,1)}, bf16[1024,4,64]{0,2,1:T(8,128)(2,1)S(1)}, u32[]{:S(2)}) copy-start(bf16[1024,4,64]{0,2,1:T(8,128)(2,1)S(1)} %get-tuple-element.1085) | copy-start | bytes 1572868
  309.3 55.7 %copy-start.17 = (bf16[1024,4,64]{0,2,1:T(8,128)(2,1)}, bf16[1024,4,64]{0,2,1:T(8,128)(2,1)S(1)}, u32[]{:S(2)}) copy-start(bf16[1024,4,64]{0,2,1:T(8,128)(2,1)S(1)} %get-tuple-element.1087) | copy-start | bytes 1572868
  309.3 55.7 %copy-start.50 = (s32[1024]{0:T(1024)}, s32[1024]{0:T(1024)S(1)}, u32[]{:S(2)}) copy-start(s32[1024]{0:T(1024)S(1)} %get-tuple-element.1096) | copy-start | bytes 12292
  350.9 39.3 %all-to-all-start.1 = ((bf16[8,128,256]{2,1,0:T(8,128)(2,1)}), bf16[8,128,256]{2,1,0:T(8,128)(2,1)}, u32[]{:S(2)}, u32[]{:S(2)}) async-start(bf16[8,128,256]{2,1,0:T(8,128)(2,1)} %bitcast.23), calls=%async_computation.1 | async-start | bytes 1048576 | tf_op jit(solution)/shard_map/all_to_all | solution.py:275
  390.2 39.3 %copy-start.52 = (s32[1024]{0:T(1024)}, s32[1024]{0:T(1024)S(1)}, u32[]{:S(2)}) copy-start(s32[1024]{0:T(1024)S(1)} %get-tuple-element.1097) | copy-start | bytes 12292
  390.2 33.1 all-to-all-start.3
  429.5 420.4 %copy-start.9 = (f32[128,2048]{1,0:T(8,128)}, f32[128,2048]{1,0:T(8,128)S(1)}, u32[]{:S(2)}) copy-start(f32[128,2048]{1,0:T(8,128)S(1)} %get-tuple-element.650) | copy-start | bytes 3145732
  434.0 187.7 %copy-start.19 = (bf16[128,2048]{1,0:T(8,128)(2,1)}, bf16[128,2048]{1,0:T(8,128)(2,1)S(1)}, u32[]{:S(2)}) copy-start(bf16[128,2048]{1,0:T(8,128)(2,1)S(1)} %get-tuple-element.622) | copy-start | bytes 1572868
  861.1 18.7 all-to-all-start.4
  879.8 37.8 %all-to-all-start.6 = ((bf16[128,8,256]{2,0,1:T(8,128)(2,1)}), bf16[128,8,256]{2,0,1:T(8,128)(2,1)}, u32[]{:S(2)}, u32[]{:S(2)}) async-start(bf16[128,8,256]{2,0,1:T(8,128)(2,1)} %bitcast.397), calls=%async_computation.6 | async-start | bytes 1048576 | tf_op jit(solution)/shard_map/all_to_all | solution.py:301
  964.5 52.3 %all-to-all-start.7 = ((bf16[1024,3,256]{2,1,0:T(4,128)(2,1)}), bf16[1024,3,256]{2,1,0:T(4,128)(2,1)}, u32[]{:S(2)}, u32[]{:S(2)}) async-start(bf16[1024,3,256]{2,1,0:T(4,128)(2,1)} %copy.222), calls=%async_computation.7 | async-start | bytes 4194304 | tf_op jit(solution)/shard_map/all_to_all | solution.py:303
  1016.8 52.4 %all-to-all-start.5 = ((bf16[1024,3,256]{2,1,0:T(4,128)(2,1)}), bf16[1024,3,256]{2,1,0:T(4,128)(2,1)}, u32[]{:S(2)}, u32[]{:S(2)}) async-start(bf16[1024,3,256]{2,1,0:T(4,128)(2,1)} %copy.215), calls=%async_computation.5 | async-start | bytes 4194304 | tf_op jit(solution)/shard_map/all_to_all | solution.py:303
  1022.2 1845.8 %reduce-scatter.3.cloned.1.call-start = ((), (), s32[]{:S(2)}) async-start(), calls=%async_computation.15 | async-start | bytes 164364288 | tf_op jit(solution)/shard_map/reduce_scatter | solution.py:350
  1201.6 2157.8 %reduce-scatter.5.cloned.1.call-start = ((), (), s32[]{:S(2)}) async-start(), calls=%async_computation.16 | async-start | bytes 47579136 | tf_op jit(solution)/shard_map/reduce_scatter | solution.py:357
  (88 other events, 741.8 us)
Sparse Core Ops, SparseCore 0:
  11.0 158.8 all-gather.5
  172.7 111.6 all-gather.7
  287.4 188.8 all-gather.11
  479.0 142.6 all-gather.9
  624.4 142.7 all-gather.13
  1201.8 1666.2 reduce-scatter.2
  2871.0 488.4 reduce-scatter.4
where the time goes:
time: 3380 us; the launch traced here: 3370 us
  waiting for transfers between devices  2560 us (76%)
  matrix products  371 us (11%)
  other arithmetic  162 us (5%)
  local copies, waits for them, and re-layouts  115 us (3%)
  blocking collectives  92.1 us (3%)
  starting transfers between devices  44.1 us (1%)
    reduce_scatter x1, waiting for transfers between devices, local(): lax.psum_scatter(weight_terms(jnp.int32(0), D // all_count * lax.axis_siz...  1530 us
    reduce_scatter x1, waiting for transfers between devices, local(): lax.psum_scatter(dot_first(joined[7], joined[8]), ('seq', 'rows'), scatte...  483 us
    all_gather x1, waiting for transfers between devices, local(): lax.all_gather(w_gate, ('seq', 'rows'), axis=0, tiled=True)  133 us
    dot_general x10, matrix products, dot_last(): lax.dot_general(left, right, (((1,), (1,)), ((), ())), preferred_element_...  125 us
    all_gather x1, waiting for transfers between devices, local(): lax.all_gather(w_down, ('seq', 'rows'), axis=0, tiled=True)  114 us
    all_gather x1, waiting for transfers between devices, local(): lax.all_gather(w_qkv, ('seq', 'rows'), axis=0, tiled=True)  110 us
    concatenate x1, other arithmetic, weight_terms(): jnp.concatenate([dot_first(normed_one, grad_mixed), dot_first(attended, g...  103 us
    unnamed x2, blocking collectives  92.1 us
  transfers between devices with their start and end apart: 15, of which 12 were waited for; matrix products, arithmetic and copies ran while one was open for 11% of the time, Pallas kernels for 0%

commit v1 on v0

v1 whole, which is shorter than its diff:
```python
import jax
import jax.numpy as jnp
from jax import lax
from jax.experimental import pallas as pl
from jax.experimental.pallas import tpu as pltpu
from jax.sharding import Mesh, PartitionSpec as P

D = 2048
HEADS = 32
HD = 64
ROT = 16
FF = 5632
MB = 2
Z = 4

NORM_EPS = 1e-05
THETA = 10000.0
MASKED = -1e30

ALL = ("z", "x", "y", "core")
PLANE = ("x", "y", "core")
TOKENS = ("y", "core", "x")


def dot_last(left, right):
    return lax.dot_general(
        left, right, (((1,), (1,)), ((), ())), preferred_element_type=jnp.float32
    )


def dot_first(left, right):
    return lax.dot_general(
        left, right, (((0,), (0,)), ((), ())), preferred_element_type=jnp.float32
    )


def dot(left, right):
    return jnp.dot(left, right, preferred_element_type=jnp.float32)


def row_layout(lengths, row_len):
    doc_ends = jnp.cumsum(lengths, dtype=jnp.int32)
    places = jnp.arange(row_len, dtype=jnp.int32)
    passed = (places[:, None] >= doc_ends[None, :]).astype(jnp.int32)
    segment = jnp.sum(passed, axis=1, dtype=jnp.int32)
    starts = jnp.sum(passed * lengths[None, :], axis=1, dtype=jnp.int32)
    return (segment, places - starts)


def norm_forward(values, norm_gain, norm_bias):
    average = jnp.mean(values, axis=-1, keepdims=True)
    centred = values - average
    inv_dev = lax.rsqrt(jnp.mean(centred * centred, axis=-1, keepdims=True) + NORM_EPS)
    scaled = centred * inv_dev
    return (scaled * norm_gain + norm_bias, scaled, inv_dev)


def norm_backward(grad_normed, scaled, inv_dev, norm_gain):
    grad_scaled = grad_normed * norm_gain
    first_mean = jnp.mean(grad_scaled, axis=-1, keepdims=True)
    second_mean = jnp.mean(grad_scaled * scaled, axis=-1, keepdims=True)
    return inv_dev * (grad_scaled - first_mean - scaled * second_mean)


def rotary_tables(positions):
    half_rot = ROT // 2
    frequency = THETA ** (-2.0 * jnp.arange(half_rot, dtype=jnp.float32) / ROT)
    angles = positions.astype(jnp.float32)[:, None] * frequency[None, :]
    return (jnp.cos(angles)[:, None, :], jnp.sin(angles)[:, None, :])


def rotate(head_vals, cosine, sine_tab, orient):
    half_rot = ROT // 2
    low_half = head_vals[..., :half_rot]
    high_half = head_vals[..., half_rot:ROT]
    return jnp.concatenate(
        [
            low_half * cosine - orient * high_half * sine_tab,
            high_half * cosine + orient * low_half * sine_tab,
            head_vals[..., ROT:],
        ],
        axis=-1,
    )


def masked_scores(queries, keys, segment):
    places = jnp.arange(segment.shape[0], dtype=jnp.int32)
    allowed = (segment[:, None] == segment[None, :]) & (places[:, None] >= places[None, :])
    scores = jnp.einsum(
        "qhd,khd->hqk", queries, keys, preferred_element_type=jnp.float32
    ) * HD ** (-0.5)
    return jnp.where(allowed[None], scores, MASKED)


def attend_forward(queries, keys, values, segment):
    scores = masked_scores(queries, keys, segment)
    row_peak = jnp.max(scores, axis=-1, keepdims=True)
    raised = jnp.exp(scores - row_peak)
    totals = jnp.sum(raised, axis=-1, keepdims=True)
    probs_low = (raised / totals).astype(jnp.bfloat16)
    attended = jnp.einsum("hqk,khd->qhd", probs_low, values, preferred_element_type=jnp.float32)
    return (attended.astype(jnp.bfloat16), row_peak + jnp.log(totals))


def attend_backward(queries, keys, values, segment, log_totals, grad):
    scale = HD ** (-0.5)
    scores = masked_scores(queries, keys, segment)
    attn_probs = jnp.exp(scores - log_totals)
    grad_probs = jnp.einsum("qhd,khd->hqk", grad, values, preferred_element_type=jnp.float32)
    inner_sum = jnp.sum(attn_probs * grad_probs, axis=-1, keepdims=True)
    grad_scores = (attn_probs * (grad_probs - inner_sum)).astype(jnp.bfloat16)
    grad_q = jnp.einsum("hqk,khd->qhd", grad_scores, keys, preferred_element_type=jnp.float32)
    grad_k = jnp.einsum("hqk,qhd->khd", grad_scores, queries, preferred_element_type=jnp.float32)
    grad_v = jnp.einsum(
        "hqk,qhd->khd", attn_probs.astype(jnp.bfloat16), grad, preferred_element_type=jnp.float32
    )
    return (
        (grad_q * scale).astype(jnp.bfloat16).astype(jnp.float32),
        (grad_k * scale).astype(jnp.bfloat16).astype(jnp.float32),
        grad_v,
    )


def local(
    tokens,
    doc_lengths,
    ln1_gain,
    ln1_bias,
    w_qkv,
    q_bias,
    k_bias_rot,
    v_bias,
    w_out,
    ln2_gain,
    ln2_bias,
    w_gate,
    w_up,
    w_down,
    cotangent,
):
    xs, ys, cs = (lax.axis_size(name) for name in PLANE)
    z_at, x_at, y_at, c_at = (lax.axis_index(name) for name in ALL)
    plane = xs * ys * cs
    count = Z * plane
    rank = (x_at * ys + y_at) * cs + c_at
    local_len = tokens.shape[2]
    row_len = local_len * Z * xs
    rows_here = ys * cs // Z
    block = D // count
    rot_block = HEADS * ROT // count
    ff_block = FF // count
    heads_here = HEADS // plane
    strided = block == HD
    width = heads_here * HD
    ff_here = Z * ff_block

    there, back = [], []
    for z in range(Z):
        for x in range(xs):
            for r in range(ys * cs):
                source = (z * xs + x) * ys * cs + r
                target = ((r // rows_here) * xs + x) * ys * cs + (r % rows_here) * Z + z
                there.append((source, target))
                back.append((target, source))

    pieces = [ln1_gain, ln1_bias, q_bias, v_bias, ln2_gain, ln2_bias, k_bias_rot]
    packed = jnp.concatenate(
        [piece.astype(jnp.float32) for piece in pieces]
        + [doc_lengths[:, 0].astype(jnp.float32).reshape(-1)]
    )
    pack_len = -(-packed.shape[0] // 512) * 512
    packed = jnp.pad(packed, (0, pack_len - packed.shape[0])).reshape(1, -1, 128)
    small = lax.all_gather(packed, ALL, axis=0, tiled=True).reshape(count, pack_len)
    fulls = [small[:, i * block : (i + 1) * block].reshape(D) for i in range(6)]
    norm1_gain, norm1_bias, q_full, v_full, norm2_gain, norm2_bias = fulls
    k_rot = small[:, 6 * block : 6 * block + rot_block].reshape(HEADS, ROT)
    k_full = jnp.concatenate([k_rot, jnp.zeros((HEADS, HD - ROT), jnp.float32)], axis=1)
    at = 6 * block + rot_block
    lengths_all = small[: ys * cs, at : at + MB * 8].reshape(ys * cs, MB, 8).astype(jnp.int32)
    lengths = lax.dynamic_slice_in_dim(lengths_all, z_at * rows_here, rows_here, 0)

    def my_heads(full):
        if strided:
            by_rank = full.reshape(heads_here, plane, HD)
            return lax.dynamic_index_in_dim(by_rank, rank, 1, False).reshape(width)
        by_rank = full.reshape(plane, width)
        return lax.dynamic_index_in_dim(by_rank, rank, 0, False)

    bias_here = jnp.concatenate([my_heads(q_full), my_heads(k_full), my_heads(v_full)])

    if strided:
        cut_qkv = w_qkv.reshape(block, 3, heads_here, plane, HD).transpose(3, 0, 1, 2, 4)
    else:
        cut_qkv = w_qkv.reshape(block, 3, plane, heads_here, HD).transpose(2, 0, 1, 3, 4)
    cut_qkv = cut_qkv.reshape(plane, block, 3 * width)

    def cut_ff(weight):
        cut = weight.reshape(block, Z, plane, ff_block).transpose(2, 0, 1, 3)
        return cut.reshape(plane, block, ff_here)

    cut_gu = jnp.concatenate([cut_ff(w_gate), cut_ff(w_up)], axis=2)
    here_qkv = lax.all_to_all(cut_qkv, PLANE, 0, 0, tiled=True).reshape(plane * block, 3 * width)
    here_gu = lax.all_to_all(cut_gu, PLANE, 0, 0, tiled=True).reshape(plane * block, 2 * ff_here)
    col_qkv = lax.all_gather(here_qkv, "z", axis=0, tiled=True)
    if strided:
        row_out = lax.all_gather(w_out, "z", axis=0, tiled=True)
    else:
        row_out = lax.dynamic_slice_in_dim(
            lax.all_gather(w_out, ALL, axis=0, tiled=True), rank * width, width, 0
        )
    col_gu = lax.all_gather(here_gu, "z", axis=0, tiled=True)
    row_down = lax.all_gather(w_down, "z", axis=0, tiled=True)

    tokens_here = lax.ppermute(tokens[:, 0], ALL, there)
    cot_here = lax.ppermute(cotangent[:, 0], ALL, there)

    def gather(chunk):
        return lax.all_gather(chunk, TOKENS, axis=0, tiled=True)

    def scatter(partial):
        return lax.psum_scatter(
            partial.astype(jnp.bfloat16), TOKENS, scatter_dimension=0, tiled=True
        ).astype(jnp.float32)

    outputs, grads_in, kept = [], [], []
    small_sums = None
    for m in range(MB):
        layouts = [row_layout(lengths[row, m], row_len) for row in range(rows_here)]
        tables = [rotary_tables(positions) for _, positions in layouts]
        chunk = tokens_here[m].astype(jnp.float32)
        normed_one, scaled_one, inv_one = norm_forward(chunk, norm1_gain, norm1_bias)
        all_one = gather(normed_one.astype(jnp.bfloat16))
        all_cot = gather(cot_here[m])
        mixed = (dot(all_one, col_qkv) + bias_here).reshape(
            rows_here, row_len, 3, heads_here, HD
        )
        heads, attended = [], []
        for row in range(rows_here):
            cosine, sine_tab = tables[row]
            queries = rotate(mixed[row, :, 0], cosine, sine_tab, 1.0).astype(jnp.bfloat16)
            keys = rotate(mixed[row, :, 1], cosine, sine_tab, 1.0).astype(jnp.bfloat16)
            values = mixed[row, :, 2].astype(jnp.bfloat16)
            segment = layouts[row][0]
            result, log_totals = attend_forward(queries, keys, values, segment)
            heads.append((queries, keys, values, segment, log_totals))
            attended.append(result.reshape(row_len, width))
        attended = jnp.concatenate(attended, axis=0)
        residual = chunk + scatter(dot(attended, row_out))
        normed_two, scaled_two, inv_two = norm_forward(residual, norm2_gain, norm2_bias)
        all_two = gather(normed_two.astype(jnp.bfloat16))
        gate_up = dot(all_two, col_gu)
        gate, up_proj = gate_up[:, :ff_here], gate_up[:, ff_here:]
        sigmoid_gate = jax.nn.sigmoid(gate)
        silu_gate = gate * sigmoid_gate
        hidden = (silu_gate * up_proj).astype(jnp.bfloat16)
        outputs.append((residual + scatter(dot(hidden, row_down))).astype(jnp.bfloat16))
        grad_hidden = dot_last(all_cot, row_down)
        grad_gate = grad_hidden * up_proj * sigmoid_gate * (1.0 + gate * (1.0 - sigmoid_gate))
        grad_gu = jnp.concatenate(
            [grad_gate.astype(jnp.bfloat16), (grad_hidden * silu_gate).astype(jnp.bfloat16)],
            axis=1,
        )
        grad_two = scatter(dot_last(grad_gu, col_gu))
        grad_residual = cot_here[m].astype(jnp.float32) + norm_backward(
            grad_two, scaled_two, inv_two, norm2_gain
        )
        all_branch = gather(grad_residual.astype(jnp.bfloat16))
        grad_attended = dot_last(all_branch, row_out).astype(jnp.bfloat16)
        grad_attended = grad_attended.reshape(rows_here, row_len, heads_here, HD)
        grad_mixed = []
        for row in range(rows_here):
            cosine, sine_tab = tables[row]
            grad_q, grad_k, grad_v = attend_backward(*heads[row], grad_attended[row])
            grad_q = rotate(grad_q, cosine, sine_tab, -1.0)
            grad_k = rotate(grad_k, cosine, sine_tab, -1.0)
            stacked = jnp.stack([grad_q, grad_k, grad_v], axis=1).astype(jnp.bfloat16)
            grad_mixed.append(stacked.reshape(row_len, 3 * width))
        grad_mixed = jnp.concatenate(grad_mixed, axis=0)
        grad_one = scatter(dot_last(grad_mixed, col_qkv))
        grads_in.append(
            (grad_residual + norm_backward(grad_one, scaled_one, inv_one, norm1_gain)).astype(
                jnp.bfloat16
            )
        )
        sums = [
            jnp.sum(grad_one * scaled_one, axis=0),
            jnp.sum(grad_one, axis=0),
            jnp.sum(grad_two * scaled_two, axis=0),
            jnp.sum(grad_two, axis=0),
            jnp.sum(grad_mixed.astype(jnp.float32), axis=0),
        ]
        small_sums = sums if m == 0 else [a + b for a, b in zip(small_sums, sums)]
        kept.append((all_one, grad_mixed, attended, all_branch, all_two, grad_gu, hidden, all_cot))

    joined = [jnp.concatenate(parts, axis=0) for parts in zip(*kept)]

    def over_z(term):
        return lax.psum_scatter(
            term.astype(jnp.bfloat16), "z", scatter_dimension=0, tiled=True
        )

    share_down = over_z(dot_first(joined[6], joined[7])).astype(jnp.float32)
    share_gu = over_z(dot_first(joined[4], joined[5])).reshape(plane, block, 2 * ff_here)
    grad_out = dot_first(joined[2], joined[3])
    if strided:
        share_out = over_z(grad_out).astype(jnp.float32)
    else:
        placed = lax.dynamic_update_slice_in_dim(
            jnp.zeros((D, D), jnp.float32), grad_out, rank * width, 0
        )
        share_out = lax.psum_scatter(
            placed.astype(jnp.bfloat16), ALL, scatter_dimension=0, tiled=True
        ).astype(jnp.float32)
    share_qkv = over_z(dot_first(joined[0], joined[1])).reshape(plane, block, 3 * width)
    share_gu = lax.all_to_all(share_gu, PLANE, 0, 0, tiled=True).astype(jnp.float32)
    share_qkv = lax.all_to_all(share_qkv, PLANE, 0, 0, tiled=True).astype(jnp.float32)

    def join_ff(part):
        return part.reshape(plane, block, Z, ff_block).transpose(1, 2, 0, 3).reshape(block, FF)

    share_gate = join_ff(share_gu[:, :, :ff_here])
    share_up = join_ff(share_gu[:, :, ff_here:])
    if strided:
        share_qkv = share_qkv.reshape(plane, block, 3, heads_here, HD).transpose(1, 2, 3, 0, 4)
    else:
        share_qkv = share_qkv.reshape(plane, block, 3, heads_here, HD).transpose(1, 2, 0, 3, 4)
    share_qkv = share_qkv.reshape(block, 3 * D)

    mine = (jnp.arange(plane) == rank).astype(jnp.float32)

    def spread(part):
        if strided:
            whole = part.reshape(heads_here, 1, HD) * mine[None, :, None]
        else:
            whole = part.reshape(1, heads_here, HD) * mine[:, None, None]
        return whole.reshape(HEADS, HD)

    mixed_sums = small_sums[4].reshape(3, width)
    k_sums = spread(mixed_sums[1])[:, :ROT]
    terms = [
        small_sums[0].reshape(count, block),
        small_sums[1].reshape(count, block),
        spread(mixed_sums[0]).reshape(count, block),
        spread(mixed_sums[2]).reshape(count, block),
        small_sums[2].reshape(count, block),
        small_sums[3].reshape(count, block),
        k_sums.reshape(count, rot_block),
    ]
    packed = jnp.concatenate(terms, axis=1)
    packed = jnp.pad(packed, ((0, 0), (0, pack_len - packed.shape[1])))
    shares = lax.psum_scatter(
        packed.reshape(count, -1, 128), ALL, scatter_dimension=0, tiled=True
    ).reshape(pack_len)
    small_shares = [shares[i * block : (i + 1) * block] for i in range(6)]
    share_k = shares[6 * block : 6 * block + rot_block]

    output = lax.ppermute(jnp.stack(outputs), ALL, back)[:, None]
    grad_tokens = lax.ppermute(jnp.stack(grads_in), ALL, back)[:, None]
    return (
        output,
        grad_tokens,
        small_shares[0],
        small_shares[1],
        share_qkv,
        small_shares[2],
        share_k,
        small_shares[3],
        share_out,
        small_shares[4],
        small_shares[5],
        share_gate,
        share_up,
        share_down,
    )


TOK = 128
N_TOK = 8
VMEM_BYTES = 56 * 2**20
ANY_SPEC = pl.BlockSpec(memory_space=pl.ANY)
VMEM_SPEC = pl.BlockSpec(memory_space=pltpu.VMEM)
DMA = pltpu.SemaphoreType.DMA


def remote(src, dst, sends, recvs, index, device):
    return pltpu.make_async_remote_copy(
        src_ref=src,
        dst_ref=dst,
        send_sem=sends.at[index],
        recv_sem=recvs.at[index],
        device_id=device,
        device_id_type=pl.DeviceIdType.MESH,
    )


class Place:
    def __init__(self):
        self.z, self.x, self.y, self.c = (lax.axis_index(name) for name in ALL)
        self.ox, self.oy, self.oc = 1 - self.x, 1 - self.y, 1 - self.c
        self.px = (self.z, self.ox, self.y, self.c)
        self.py = (self.z, self.x, self.oy, self.c)
        self.ps = (self.z, self.x, self.y, self.oc)
        self.rank = (self.x * 2 + self.y) * 2 + self.c

        self.partners = [(2 * self.c + j, self.x, self.y, self.z // 2) for j in range(2)]
        self.apart = [self.z != 2 * self.c + j for j in range(2)]


def greet(devices, place=None):
    barrier = pltpu.get_barrier_semaphore()
    for device in devices:
        pl.semaphore_signal(
            barrier, inc=1, device_id=device, device_id_type=pl.DeviceIdType.MESH
        )
    extra = 0
    if place is not None:
        for j in range(2):
            extra = extra + lax.select(place.apart[j], 1, 0)

            @pl.when(place.apart[j])
            def _():
                pl.semaphore_signal(
                    barrier,
                    inc=1,
                    device_id=place.partners[j],
                    device_id_type=pl.DeviceIdType.MESH,
                )

    pl.semaphore_wait(barrier, len(devices) + extra)


def hop(src, dst, send, recv, device):
    return pltpu.make_async_remote_copy(
        src_ref=src,
        dst_ref=dst,
        send_sem=send,
        recv_sem=recv,
        device_id=device,
        device_id_type=pl.DeviceIdType.MESH,
    )


def hop_start(apart, src, dst, send, recv, device):
    @pl.when(apart)
    def _():
        hop(src, dst, send, recv, device).start()

    @pl.when(jnp.logical_not(apart))
    def _():
        pltpu.make_async_copy(src, dst, recv).start()


def hop_landed(apart, spot, send, recv, device):
    @pl.when(apart)
    def _():
        hop(spot, spot, send, recv, device).wait_recv()

    @pl.when(jnp.logical_not(apart))
    def _():
        pltpu.make_async_copy(spot, spot, recv).wait()


def hop_sent(apart, src, send, recv, device):
    @pl.when(apart)
    def _():
        hop(src, src, send, recv, device).wait_send()


class MoveIn:
    def __init__(self, place, src, out, swap, sends, recvs):
        self.place, self.src, self.out, self.swap = place, src, out, swap
        self.sends, self.recvs = sends, recvs
        z, x, y, c = place.z, place.x, place.y, place.c
        self.slot = z % 2
        self.mine = (2 * c + y, x, y, z // 2)
        self.other = (2 * c + 1 - y, x, y, z // 2)
        self.mine_apart = z != 2 * c + y
        self.other_apart = z != 2 * c + 1 - y

    def start(self):
        y, recv = self.place.y, self.recvs.at[self.slot]
        across = self.src.at[1 - y]
        hop(across, self.swap, self.sends.at[2], self.recvs.at[2], self.place.py).start()
        hop_start(
            self.mine_apart, self.src.at[y], self.out.at[self.slot], self.sends.at[0], recv, self.mine
        )

    def middle(self):
        recv = self.recvs.at[self.slot]
        hop(self.swap, self.swap, self.sends.at[2], self.recvs.at[2], self.place.py).wait_recv()
        hop_start(
            self.other_apart, self.swap, self.out.at[self.slot], self.sends.at[1], recv, self.other
        )

    def finish(self):
        place, recv = self.place, self.recvs.at[self.slot]
        for j in range(2):
            hop_landed(
                place.apart[j], self.out.at[j], self.sends.at[j], self.recvs.at[j], place.partners[j]
            )
        hop_sent(self.mine_apart, self.src.at[place.y], self.sends.at[0], recv, self.mine)
        hop_sent(self.other_apart, self.swap, self.sends.at[1], recv, self.other)
        hop(self.swap, self.swap, self.sends.at[2], self.recvs.at[2], place.py).wait_send()


class MoveBack:
    def __init__(self, place, own, out, swap, sends, recvs):
        self.place, self.own, self.out, self.swap = place, own, out, swap
        self.sends, self.recvs = sends, recvs
        self.slot = place.z % 2

    def half(self, h):
        return pl.ds(h * (TOK // 2), TOK // 2)

    def start(self):
        place = self.place
        for h in range(2):
            rows = self.half(h)
            recv = self.recvs.at[2 * self.slot + h]
            for j in range(2):
                for straight in (True, False):
                    dst = self.out.at[place.y, rows] if straight else self.swap.at[rows]

                    @pl.when((place.y == self.slot) == straight)
                    def _():
                        hop_start(
                            place.apart[j],
                            self.own.at[j, rows],
                            dst,
                            self.sends.at[2 * j + h],
                            recv,
                            place.partners[j],
                        )

    def landed(self, index, h, spot):
        place = self.place
        device = (2 * place.c + index, place.x, place.y, place.z // 2)
        apart = place.z != 2 * place.c + index
        hop_landed(apart, spot, self.sends.at[h], self.recvs.at[2 * index + h], device)

    def middle(self):
        place = self.place
        for h in range(2):
            rows = self.half(h)
            self.landed(1 - place.y, h, self.swap.at[rows])
            hop(
                self.swap.at[rows],
                self.out.at[place.y, rows],
                self.sends.at[4 + h],
                self.recvs.at[4 + h],
                place.py,
            ).start()

    def finish(self):
        place = self.place
        for h in range(2):
            rows = self.half(h)
            self.landed(place.y, h, self.out.at[place.y, rows])
            spot = self.out.at[1 - place.y, rows]
            hop(spot, spot, self.sends.at[4 + h], self.recvs.at[4 + h], place.py).wait_recv()
            for j in range(2):
                hop_sent(
                    place.apart[j],
                    self.own.at[j, rows],
                    self.sends.at[2 * j + h],
                    self.recvs.at[2 * self.slot + h],
                    place.partners[j],
                )
            hop(
                self.swap.at[rows],
                self.swap.at[rows],
                self.sends.at[4 + h],
                self.recvs.at[4 + h],
                place.py,
            ).wait_send()


MOVE_SCRATCH = [pltpu.VMEM((TOK, D), jnp.bfloat16), DMA((6,)), DMA((6,))]
WHOLE = (2, 2, 2, 2, TOK)


class Gather:
    def __init__(self, place, own, out, sends, recvs):
        self.place, self.own, self.out = place, own, out
        self.sends, self.recvs = sends, recvs
        x, y, ox, oy = place.x, place.y, place.ox, place.oy
        self.me, self.by_x, self.by_y, self.far = (x, y), (ox, y), (x, oy), (ox, oy)
        self.started, self.keep = [], []

    def spot(self, j, chip, core):
        return self.out.at[chip[1], core, j, chip[0]]

    def go(self, src, j, chip, index, device):
        dst = self.spot(j, chip, self.place.c)
        copy = remote(src, dst, self.sends, self.recvs, index, device)
        copy.start()
        self.started.append(copy)

    def landed(self, j, chip, index, device, core=None):
        spot = self.spot(j, chip, self.place.c if core is None else core)
        remote(spot, spot, self.sends, self.recvs, index, device).wait_recv()
        return spot

    def send(self, j):
        place, own, me = self.place, self.own.at[j], self.me
        if j == 0:
            self.go(own, 0, me, 0, place.px)
            self.go(own, 0, me, 3, place.py)
        else:
            self.go(own, 1, me, 1, place.py)
            self.go(own, 1, me, 2, place.px)
        self.go(own, j, me, 6 + j, place.ps)
        copy = pltpu.make_async_copy(own, self.spot(j, me, place.c), self.sends.at[14 + j])
        copy.start()
        self.keep.append(copy)

    def relay(self):
        place = self.place
        spot = self.landed(0, self.by_x, 0, place.px)
        self.go(spot, 0, self.by_x, 5, place.py)
        self.go(spot, 0, self.by_x, 9, place.ps)
        spot = self.landed(1, self.by_y, 1, place.py)
        self.go(spot, 1, self.by_y, 4, place.px)
        self.go(spot, 1, self.by_y, 8, place.ps)

    def hand_over(self):
        place = self.place
        spot = self.landed(0, self.by_y, 3, place.py)
        self.go(spot, 0, self.by_y, 11, place.ps)
        spot = self.landed(1, self.by_x, 2, place.px)
        self.go(spot, 1, self.by_x, 10, place.ps)

    def hand_over_far(self):
        place = self.place
        spot = self.landed(0, self.far, 5, place.py)
        self.go(spot, 0, self.far, 13, place.ps)
        spot = self.landed(1, self.far, 4, place.px)
        self.go(spot, 1, self.far, 12, place.ps)

    def finish(self):
        for j, chip, index in (
            (0, self.me, 6),
            (1, self.me, 7),
            (1, self.by_y, 8),
            (0, self.by_x, 9),
            (1, self.by_x, 10),
            (0, self.by_y, 11),
            (1, self.far, 12),
            (0, self.far, 13),
        ):
            self.landed(j, chip, index, self.place.ps, self.place.oc)
        for copy in self.keep:
            copy.wait()
        for copy in self.started:
            copy.wait_send()

    def steps(self):
        self.send(0)
        self.send(1)
        yield
        self.relay()
        yield
        self.hand_over()
        yield
        self.hand_over_far()
        yield
        self.finish()


GATHER_SEMS = 16
SUM_SEMS = 10
SUM_SCRATCH = [
    pltpu.VMEM((4, 2, TOK, D), jnp.bfloat16),
    pltpu.VMEM((4, 2, TOK, D), jnp.bfloat16),
    pltpu.VMEM((4, 2, TOK, D), jnp.float32),
    pltpu.VMEM((2, TOK, D), jnp.bfloat16),
    pltpu.VMEM((6, TOK, D), jnp.bfloat16),
    pltpu.VMEM((4, TOK, D), jnp.bfloat16),
    DMA((SUM_SEMS,)),
    DMA((SUM_SEMS,)),
]
COLUMNS = 512


def plane_sum(place, acts, weight, turned, scratch, finish, idle=None):
    to_sib, from_sib, mine, through, onward, final, sends, recvs = scratch
    x, y, c = place.x, place.y, place.c

    def times(tx, ty, core, store):
        left = acts[ty, core, :, tx].reshape(2 * TOK, acts.shape[-1])

        def tile(j, _):
            cols = pl.ds(pl.multiple_of(j * COLUMNS, COLUMNS), COLUMNS)
            if turned:
                result = dot_last(left, weight[cols, :])
            else:
                result = dot(left, weight[:, cols])
            store(cols, result.reshape(2, TOK, COLUMNS))
            return 0

        lax.fori_loop(0, D // COLUMNS, tile, 0)

    places = ((place.ox, place.oy), (place.ox, y), (x, place.oy), (x, y))

    def products(q):
        tx, ty = places[q]

        def keep_out(cols, result):
            to_sib[q, :, :, cols] = result.astype(jnp.bfloat16)

        def keep_in(cols, result):
            mine[q, :, :, cols] = result

        times(tx, ty, place.oc, keep_out)
        copy = remote(to_sib.at[q], from_sib.at[q], sends, recvs, q, place.ps)
        copy.start()
        times(tx, ty, c, keep_in)
        copy.wait()

    def chip(q, m):
        return mine[q, m] + from_sib[q, m].astype(jnp.float32)

    def go(src, dst, index, device):
        copy = remote(src, dst, sends, recvs, index, device)
        copy.start()
        return copy

    def landed(spot, index, device):
        remote(spot, spot, sends, recvs, index, device).wait_recv()

    started = []
    products(0)
    onward[0] = chip(0, 0).astype(jnp.bfloat16)
    started.append(go(onward.at[0], through.at[0], 4, place.px))
    onward[1] = chip(0, 1).astype(jnp.bfloat16)
    started.append(go(onward.at[1], through.at[1], 5, place.py))
    products(1)
    onward[2] = chip(1, 0).astype(jnp.bfloat16)
    started.append(go(onward.at[2], final.at[0], 6, place.px))
    products(2)
    landed(through.at[0], 4, place.px)
    onward[5] = (chip(2, 0) + through[0].astype(jnp.float32)).astype(jnp.bfloat16)
    started.append(go(onward.at[5], final.at[2], 9, place.py))
    onward[3] = chip(2, 1).astype(jnp.bfloat16)
    started.append(go(onward.at[3], final.at[3], 7, place.py))
    landed(through.at[1], 5, place.py)
    onward[4] = (chip(1, 1) + through[1].astype(jnp.float32)).astype(jnp.bfloat16)
    started.append(go(onward.at[4], final.at[1], 8, place.px))
    products(3)
    if idle is not None:
        idle()

    def total(m):
        return chip(3, m) + final[m].astype(jnp.float32) + final[2 + m].astype(jnp.float32)

    landed(final.at[0], 6, place.px)
    landed(final.at[2], 9, place.py)
    finish(0, total(0))
    if idle is not None:
        idle()
    landed(final.at[1], 8, place.px)
    landed(final.at[3], 7, place.py)
    finish(1, total(1))
    for copy in started:
        copy.wait_send()


def sum_steps(place, parts, result, scratch):
    from_sib, mine, through, onward, final, sends, recvs, loads = scratch
    x, y, c = place.x, place.y, place.c
    places = ((place.ox, place.oy), (place.ox, y), (x, place.oy), (x, y))
    to_sib, local = [], []
    for q, (tx, ty) in enumerate(places):
        source = parts.at[ty, place.oc, :, tx]
        copy = remote(source, from_sib.at[q], sends, recvs, q, place.ps)
        copy.start()
        to_sib.append(copy)
        copy = pltpu.make_async_copy(parts.at[ty, c, :, tx], mine.at[q], loads.at[q])
        copy.start()
        local.append(copy)

    def chip(q, m):
        return mine[q, m].astype(jnp.float32) + from_sib[q, m].astype(jnp.float32)

    def sib_landed(q):
        to_sib[q].wait()
        local[q].wait()

    def go(src, dst, index, device):
        copy = remote(src, dst, sends, recvs, index, device)
        copy.start()
        return copy

    def landed(spot, index, device):
        remote(spot, spot, sends, recvs, index, device).wait_recv()

    started = []
    yield
    sib_landed(0)
    onward[0] = chip(0, 0).astype(jnp.bfloat16)
    started.append(go(onward.at[0], through.at[0], 4, place.px))
    onward[1] = chip(0, 1).astype(jnp.bfloat16)
    started.append(go(onward.at[1], through.at[1], 5, place.py))
    sib_landed(1)
    onward[2] = chip(1, 0).astype(jnp.bfloat16)
    started.append(go(onward.at[2], final.at[0], 6, place.px))
    sib_landed(2)
    onward[3] = chip(2, 1).astype(jnp.bfloat16)
    started.append(go(onward.at[3], final.at[3], 7, place.py))
    yield
    landed(through.at[1], 5, place.py)
    onward[4] = (chip(1, 1) + through[1].astype(jnp.float32)).astype(jnp.bfloat16)
    started.append(go(onward.at[4], final.at[1], 8, place.px))
    landed(through.at[0], 4, place.px)
    onward[5] = (chip(2, 0) + through[0].astype(jnp.float32)).astype(jnp.bfloat16)
    started.append(go(onward.at[5], final.at[2], 9, place.py))
    sib_landed(3)
    yield
    landed(final.at[0], 6, place.px)
    landed(final.at[3], 7, place.py)
    landed(final.at[1], 8, place.px)
    landed(final.at[2], 9, place.py)
    for copy in started:
        copy.wait_send()
    for m in range(2):
        result(
            m, chip(3, m) + final[m].astype(jnp.float32) + final[2 + m].astype(jnp.float32)
        )


STEP_SCRATCH = [
    pltpu.VMEM((4, 2, TOK, D), jnp.bfloat16),
    pltpu.VMEM((4, 2, TOK, D), jnp.bfloat16),
    pltpu.VMEM((2, TOK, D), jnp.bfloat16),
    pltpu.VMEM((6, TOK, D), jnp.bfloat16),
    pltpu.VMEM((4, TOK, D), jnp.bfloat16),
    DMA((SUM_SEMS,)),
    DMA((SUM_SEMS,)),
    DMA((4,)),
]


def kernel_call(body, out_shape, out_specs, in_specs, scratch, ident, args):
    return pl.pallas_call(
        body,
        out_shape=out_shape,
        in_specs=in_specs,
        out_specs=out_specs,
        scratch_shapes=scratch,
        compiler_params=pltpu.CompilerParams(
            collective_id=ident, has_side_effects=True, vmem_limit_bytes=VMEM_BYTES
        ),
    )(*args)


def shape(dims, kind=jnp.bfloat16):
    return jax.ShapeDtypeStruct(dims, kind)


def plane_peers(place):
    peers = []
    for k in range(1, 8):
        dx, dy, dc = k // 4, k // 2 % 2, k % 2
        px, py, pc = (place.x + dx) % 2, (place.y + dy) % 2, (place.c + dc) % 2
        peers.append(((place.z, px, py, pc), (px * 2 + py) * 2 + pc))
    return peers


def z_peers(place):
    return [((place.z + j) % Z, place.x, place.y, place.c) for j in range(1, Z)]


def exchange_start(place, src, dst, sends, recvs, base):
    me = place.rank
    own = pltpu.make_async_copy(src.at[me], dst.at[me], sends.at[base])
    own.start()
    started = []
    for k, (device, rank) in enumerate(plane_peers(place)):
        copy = remote(src.at[rank], dst.at[me], sends, recvs, base + 1 + k, device)
        copy.start()
        started.append(copy)
    return own, started


def exchange_wait(place, own, started, dst, sends, recvs, base):
    own.wait()
    for k, (device, rank) in enumerate(plane_peers(place)):
        spot = dst.at[rank]
        remote(spot, spot, sends, recvs, base + 1 + k, device).wait_recv()
    for copy in started:
        copy.wait_send()


PACK_ROWS = 16
HALF = 64


def prologue(w_qkv, tokens, pieces, lengths):
    heads_here = WIDTH // HD

    def body(qkv_ref, tok_ref, *refs):
        piece_refs, len_ref = refs[: len(pieces)], refs[len(pieces)]
        qkv_out, tok_out, vec_out, bias_out, len_out = refs[len(pieces) + 1 : len(pieces) + 6]
        packed, small, cut, sends, recvs, *swap = refs[len(pieces) + 6 :]
        place = Place()
        peers = plane_peers(place)
        others = z_peers(place)
        packed[...] = jnp.zeros_like(packed)
        for i, ref in enumerate(piece_refs):
            packed[i : i + 1, : ref.shape[1]] = ref[...].astype(jnp.float32)
        packed[8 : 8 + MB, :8] = len_ref[...].astype(jnp.float32)
        greet([device for device, _ in peers] + others, place)
        move = MoveIn(place, tok_ref, tok_out, *swap)
        move.start()
        me, z = place.rank, place.z
        own = pltpu.make_async_copy(packed, small.at[me, z], sends.at[1])
        own.start()
        first = []
        for j, device in enumerate(others):
            copy = remote(packed, small.at[me, z], sends, recvs, 2 + j, device)
            copy.start()
            first.append(copy)
        for p in range(8):
            columns = []
            for k in range(3):
                for at in range(heads_here):
                    lane = (k * HEADS + at * 8 + p) * HD
                    columns.append(qkv_ref[:, lane : lane + HD])
            cut[p] = jnp.concatenate(columns, axis=1)
        qkv = exchange_start(place, cut, qkv_out, sends, recvs, 16)
        move.middle()
        own.wait()
        for j, device in enumerate(others):
            spot = small.at[me, (z + Z - 1 - j) % Z]
            remote(spot, spot, sends, recvs, 2 + j, device).wait_recv()
        second = []
        for k, (device, rank) in enumerate(peers):
            copy = remote(small.at[me], small.at[me], sends, recvs, 8 + k, device)
            copy.start()
            second.append(copy)
        for k, (device, rank) in enumerate(peers):
            spot = small.at[rank]
            remote(spot, spot, sends, recvs, 8 + k, device).wait_recv()
        for at in range(Z):
            for p in range(0, 8, 2):
                both = [small[p, at, :8, :HALF], small[p + 1, at, :8, :HALF]]
                lane = (at * 8 + p) * HALF
                vec_out[:, lane : lane + 2 * HALF] = jnp.concatenate(both, axis=1)
        for k, row in enumerate((2, 6, 3)):
            for at in range(0, Z, 2):
                both = [small[me, at + j, row : row + 1, :HALF] for j in range(2)]
                lane = (k * Z + at) * HALF
                bias_out[:, lane : lane + 2 * HALF] = jnp.concatenate(both, axis=1)
        my_row = (z % 2) * 2 + z // 2
        len_out[...] = small[my_row, 0, 8 : 8 + MB, :8].astype(jnp.int32)
        for copy in first + second:
            copy.wait_send()
        exchange_wait(place, *qkv, qkv_out, sends, recvs, 16)
        move.finish()

    return kernel_call(
        body,
        (
            shape((8, w_qkv.shape[0], 3 * WIDTH)),
            shape(tokens.shape),
            shape((8, D), jnp.float32),
            shape((1, 3 * WIDTH), jnp.float32),
            shape((MB, 8), jnp.int32),
        ),
        [ANY_SPEC] * 2 + [VMEM_SPEC] * 3,
        [VMEM_SPEC, ANY_SPEC] + [VMEM_SPEC] * (len(pieces) + 1),
        [
            pltpu.VMEM((PACK_ROWS, 128), jnp.float32),
            pltpu.VMEM((8, Z, PACK_ROWS, 128), jnp.float32),
            pltpu.VMEM((8, w_qkv.shape[0], 3 * WIDTH), jnp.bfloat16),
            DMA((24,)),
            DMA((24,)),
        ]
        + MOVE_SCRATCH,
        0,
        (w_qkv, tokens, *pieces, lengths),
    )


def kernel_norm(values):
    average = jnp.mean(values, axis=-1, keepdims=True)
    centred = values - average
    inv_dev = lax.rsqrt(jnp.mean(centred * centred, axis=-1, keepdims=True) + NORM_EPS)
    return centred * inv_dev, inv_dev


FF_HERE = 704
FF_MAIN = 640
FF_BLOCK = 176


def first_gather(tokens, vectors, w_gate, w_up, cot):
    rows = w_gate.shape[0]

    def body(
        tok_ref, vec_ref, gate_ref, up_ref, cot_ref, one_out, gu_out, cot_out,
        own, cut, sends, recvs, gu_sends, gu_recvs, *swap,
    ):
        place = Place()
        for m in range(2):
            scaled, _ = kernel_norm(tok_ref[m].astype(jnp.float32))
            own[m] = (scaled * vec_ref[0:1, :] + vec_ref[1:2, :]).astype(jnp.bfloat16)
        greet([device for device, _ in plane_peers(place)], place)
        move = MoveIn(place, cot_ref, cot_out, *swap)
        move.start()
        steps = Gather(place, own, one_out, sends, recvs).steps()
        advance(steps)
        for p in range(8):

            def columns(ref):
                starts = [(at * 8 + p) * FF_BLOCK for at in range(Z)]
                return jnp.concatenate([ref[:, lane : lane + FF_BLOCK] for lane in starts], axis=1)

            gate, up = columns(gate_ref), columns(up_ref)
            cut[p, :, :FF_MAIN] = gate[:, :FF_MAIN]
            cut[p, :, FF_MAIN : 2 * FF_MAIN] = up[:, :FF_MAIN]
            cut[p, :, 2 * FF_MAIN :] = jnp.concatenate([gate[:, FF_MAIN:], up[:, FF_MAIN:]], axis=1)
        local, started = exchange_start(place, cut, gu_out, gu_sends, gu_recvs, 0)
        move.middle()
        for _ in steps:
            pass
        exchange_wait(place, local, started, gu_out, gu_sends, gu_recvs, 0)
        move.finish()

    return kernel_call(
        body,
        (shape(WHOLE + (D,)), shape((8, rows, 2 * FF_HERE)), shape(cot.shape)),
        [ANY_SPEC] * 3,
        [VMEM_SPEC] * 4 + [ANY_SPEC],
        [
            pltpu.VMEM((2, TOK, D), jnp.bfloat16),
            pltpu.VMEM((8, rows, 2 * FF_HERE), jnp.bfloat16),
            DMA((GATHER_SEMS,)),
            DMA((GATHER_SEMS,)),
            DMA((8,)),
            DMA((8,)),
        ]
        + MOVE_SCRATCH,
        1,
        (tokens, vectors, w_gate, w_up, cot),
    )


def out_projection(attended, row_out, tokens, vectors):
    def body(
        act_ref, weight_ref, tok_ref, vec_ref, res_out, two_out, own, sends, recvs, *scratch,
    ):
        place = Place()
        greet([place.px, place.py, place.ps])
        gather = Gather(place, own, two_out, sends, recvs)

        def finish(m, total):
            residual = tok_ref[m].astype(jnp.float32) + total
            res_out[m] = residual
            scaled, _ = kernel_norm(residual)
            own[m] = (scaled * vec_ref[4:5, :] + vec_ref[5:6, :]).astype(jnp.bfloat16)
            gather.send(m)

        plane_sum(place, act_ref, weight_ref, False, scratch, finish)
        gather.relay()
        gather.hand_over()
        gather.hand_over_far()
        gather.finish()

    return kernel_call(
        body,
        (shape((2, TOK, D), jnp.float32), shape(WHOLE + (D,))),
        [VMEM_SPEC, ANY_SPEC],
        [VMEM_SPEC] * 4,
        [
            pltpu.VMEM((2, TOK, D), jnp.bfloat16),
            DMA((GATHER_SEMS,)),
            DMA((GATHER_SEMS,)),
        ]
        + SUM_SCRATCH,
        2,
        (attended, row_out, tokens, vectors),
    )


def norm_grad(grad, scaled, inv_dev, gain):
    grad_scaled = grad * gain
    first_mean = jnp.mean(grad_scaled, axis=-1, keepdims=True)
    second_mean = jnp.mean(grad_scaled * scaled, axis=-1, keepdims=True)
    return inv_dev * (grad_scaled - first_mean - scaled * second_mean)


def ffn_backward(grad_gu, col_gu, residual, cot, vectors, hidden, row_down):
    def body(
        act_ref, weight_ref, res_in, cot_in, vec_ref, hidden_in, down_in,
        grad_out, branch_out, sums_out, parts_out,
        own, sends, recvs, staged, part_sems, res_ref, cot_ref, hidden_ref, down_ref, load_sems,
        *scratch,
    ):
        place = Place()
        pairs = ((hidden_in, hidden_ref), (down_in, down_ref), (res_in, res_ref), (cot_in, cot_ref))
        loads = [
            pltpu.make_async_copy(src, dst, load_sems.at[i]) for i, (src, dst) in enumerate(pairs)
        ]
        for load in loads:
            load.start()
        stores = []

        def part():
            i = len(stores)
            y, c, x = i // 4, i // 2 % 2, i % 2
            if i == 0:
                for load in loads:
                    load.wait()
            if i >= 2:
                stores[i - 2].wait()
            left = hidden_ref[y, c, :, x].reshape(2 * TOK, FF_HERE)

            def tile(j, _):
                cols = pl.ds(pl.multiple_of(j * COLUMNS, COLUMNS), COLUMNS)
                result = dot(left, down_ref[:, cols]).astype(jnp.bfloat16)
                staged[i % 2, :, :, cols] = result.reshape(2, TOK, COLUMNS)
                return 0

            lax.fori_loop(0, D // COLUMNS, tile, 0)
            copy = pltpu.make_async_copy(
                staged.at[i % 2], parts_out.at[y, c, :, x], part_sems.at[i % 2]
            )
            copy.start()
            stores.append(copy)

        def two_parts():
            part()
            part()

        greet([place.px, place.py, place.ps])
        gather = Gather(place, own, branch_out, sends, recvs)

        def finish(m, grad):
            scaled, inv_dev = kernel_norm(res_ref[m])
            result = cot_ref[m].astype(jnp.float32) + norm_grad(grad, scaled, inv_dev, vec_ref[4:5, :])
            grad_out[m] = result
            own[m] = result.astype(jnp.bfloat16)
            gather.send(m)
            by_gain = jnp.sum(grad * scaled, axis=0, keepdims=True)
            by_bias = jnp.sum(grad, axis=0, keepdims=True)
            if m == 0:
                sums_out[0:1, :] = by_gain
                sums_out[1:2, :] = by_bias
            else:
                sums_out[0:1, :] += by_gain
                sums_out[1:2, :] += by_bias

        plane_sum(place, act_ref, weight_ref, True, scratch, finish, two_parts)
        two_parts()
        gather.relay()
        two_parts()
        gather.hand_over()
        gather.hand_over_far()
        gather.finish()
        for copy in stores[-2:]:
            copy.wait()

    return kernel_call(
        body,
        (
            shape((2, TOK, D), jnp.float32),
            shape(WHOLE + (D,)),
            shape((2, D), jnp.float32),
            shape(WHOLE + (D,)),
        ),
        [VMEM_SPEC, ANY_SPEC, VMEM_SPEC, ANY_SPEC],
        [VMEM_SPEC] * 2 + [ANY_SPEC] * 2 + [VMEM_SPEC] + [ANY_SPEC] * 2,
        [
            pltpu.VMEM((2, TOK, D), jnp.bfloat16),
            DMA((GATHER_SEMS,)),
            DMA((GATHER_SEMS,)),
            pltpu.VMEM((2, 2, TOK, D), jnp.bfloat16),
            DMA((2,)),
            pltpu.VMEM((2, TOK, D), jnp.float32),
            pltpu.VMEM((2, TOK, D), jnp.bfloat16),
            pltpu.VMEM(hidden.shape, jnp.bfloat16),
            pltpu.VMEM(row_down.shape, jnp.bfloat16),
            DMA((4,)),
        ]
        + SUM_SCRATCH,
        3,
        (grad_gu, col_gu, residual, cot, vectors, hidden, row_down),
    )


def input_grad(
    grad_mixed, col_qkv, tokens, grad_residual, vectors, output, share_gu, sums_two, mixed_sums
):
    rows = share_gu.shape[1]
    heads_here = WIDTH // HD

    def body(
        act_ref, weight_ref, tok_ref, grad_ref, vec_ref, output_ref, gu_ref, two_ref, mixed_ref,
        own, packed, back_out, gate_out, up_out,
        sums_one, gu_in, gu_sends, gu_recvs, swap, move_sends, move_recvs, *scratch,
    ):
        place = Place()
        greet([device for device, _ in plane_peers(place)], place)
        move = MoveBack(place, output_ref, back_out, swap, move_sends, move_recvs)
        move.start()
        local, started = exchange_start(place, gu_ref, gu_in, gu_sends, gu_recvs, 0)

        def finish(m, grad):
            scaled, inv_dev = kernel_norm(tok_ref[m].astype(jnp.float32))
            result = grad_ref[m] + norm_grad(grad, scaled, inv_dev, vec_ref[0:1, :])
            own[m] = result.astype(jnp.bfloat16)
            by_gain = jnp.sum(grad * scaled, axis=0, keepdims=True)
            by_bias = jnp.sum(grad, axis=0, keepdims=True)
            if m == 0:
                sums_one[0:1, :] = by_gain
                sums_one[1:2, :] = by_bias
            else:
                sums_one[0:1, :] += by_gain
                sums_one[1:2, :] += by_bias

        stage = []

        def lay_out():
            stage.append(len(stage))
            if stage[-1] == 1:
                move.middle()
            if stage[-1] != 0:
                return
            packed[...] = jnp.zeros_like(packed)
            for at in range(Z):
                for p in range(8):
                    lane = (at * 8 + p) * HALF
                    packed[p, at, 4:6, :HALF] = two_ref[:, lane : lane + HALF]
            mixed = mixed_ref[0] + mixed_ref[1]
            for k, row in enumerate((2, 6, 3)):
                for at in range(heads_here):
                    lane = (k * heads_here + at) * HD
                    packed[place.rank, at, row : row + 1, :HALF] = mixed[:, lane : lane + HD]
            exchange_wait(place, local, started, gu_in, gu_sends, gu_recvs, 0)
            tail_at = 2 * FF_MAIN
            tail_mid = tail_at + FF_HERE - FF_MAIN
            gates, ups = [], []
            for p in range(8):
                block = gu_in[p].astype(jnp.float32)
                gates.append(
                    jnp.concatenate([block[:, :FF_MAIN], block[:, tail_at:tail_mid]], axis=1)
                )
                ups.append(jnp.concatenate([block[:, FF_MAIN:tail_at], block[:, tail_mid:]], axis=1))
            for out, blocks in ((gate_out, gates), (up_out, ups)):
                for at in range(Z):
                    lane = at * FF_BLOCK
                    pieces = [block[:, lane : lane + FF_BLOCK] for block in blocks]
                    joined = jnp.concatenate(pieces, axis=1).astype(jnp.bfloat16)
                    out[:, at * 8 * FF_BLOCK : (at + 1) * 8 * FF_BLOCK] = joined

        plane_sum(place, act_ref, weight_ref, True, scratch, finish, lay_out)
        for at in range(Z):
            for p in range(8):
                lane = (at * 8 + p) * HALF
                packed[p, at, 0:2, :HALF] = sums_one[:, lane : lane + HALF]
        move.finish()

    return kernel_call(
        body,
        (
            shape((2, TOK, D)),
            shape((8, Z, SMALL_ROWS, 128), jnp.float32),
            shape((2, TOK, D)),
            shape((rows, FF)),
            shape((rows, FF)),
        ),
        [VMEM_SPEC, VMEM_SPEC, ANY_SPEC, VMEM_SPEC, VMEM_SPEC],
        [VMEM_SPEC] * 5 + [ANY_SPEC] * 2 + [VMEM_SPEC] * 2,
        [
            pltpu.VMEM((2, D), jnp.float32),
            pltpu.VMEM(share_gu.shape, jnp.bfloat16),
            DMA((8,)),
            DMA((8,)),
        ]
        + MOVE_SCRATCH
        + SUM_SCRATCH,
        5,
        (
            grad_mixed, col_qkv, tokens, grad_residual, vectors, output, share_gu, sums_two, mixed_sums,
        ),
    )


SMALL_ROWS = 8


def epilogue(share_qkv, grad_tokens, packed):
    rows = share_qkv.shape[1]
    heads_here = WIDTH // HD

    def body(
        qkv_ref, tok_ref, packed_ref, qkv_out, tok_out, small_out,
        qkv_in, near, half, across, sends, recvs, *swap,
    ):
        place = Place()
        peers = plane_peers(place)
        others = z_peers(place)
        me = place.rank
        greet([device for device, _ in peers] + others, place)
        move = MoveBack(place, tok_ref, tok_out, *swap)
        move.start()
        qkv = exchange_start(place, qkv_ref, qkv_in, sends, recvs, 16)
        first = []
        for k, (device, rank) in enumerate(peers):
            copy = remote(packed_ref.at[rank], near.at[k], sends, recvs, 8 + k, device)
            copy.start()
            first.append(copy)
        added = packed_ref[me]
        for k, (device, rank) in enumerate(peers):
            spot = near.at[k]
            remote(spot, spot, sends, recvs, 8 + k, device).wait_recv()
            added = added + near[k]
        half[...] = added
        for j, device in enumerate(others):
            copy = remote(half.at[device[0]], across.at[j], sends, recvs, 2 + j, device)
            copy.start()
            first.append(copy)
        move.middle()
        exchange_wait(place, *qkv, qkv_in, sends, recvs, 16)
        for k in range(3):
            for at in range(heads_here):
                lane = (k * heads_here + at) * HD
                pieces = [qkv_in[p, :, lane : lane + HD].astype(jnp.float32) for p in range(8)]
                to = (k * HEADS + at * 8) * HD
                qkv_out[:, to : to + 8 * HD] = jnp.concatenate(pieces, axis=1)
        result = half[place.z]
        for j, device in enumerate(others):
            spot = across.at[j]
            remote(spot, spot, sends, recvs, 2 + j, device).wait_recv()
            result = result + across[j]
        small_out[...] = result
        for copy in first:
            copy.wait_send()
        move.finish()

    small = (SMALL_ROWS, 128)
    return kernel_call(
        body,
        (
            shape((rows, 3 * D), jnp.float32),
            shape(grad_tokens.shape),
            shape(small, jnp.float32),
        ),
        [VMEM_SPEC, ANY_SPEC, VMEM_SPEC],
        [ANY_SPEC] * 2 + [VMEM_SPEC],
        [
            pltpu.VMEM(share_qkv.shape, jnp.bfloat16),
            pltpu.VMEM((7, Z) + small, jnp.float32),
            pltpu.VMEM((Z,) + small, jnp.float32),
            pltpu.VMEM((Z - 1,) + small, jnp.float32),
            DMA((24,)),
            DMA((24,)),
        ]
        + MOVE_SCRATCH,
        6,
        (share_qkv, grad_tokens, packed),
    )


Q_BLOCK = 256
WIDTH = 256
SCALE = HD ** (-0.5)
PROJECTED = 512


def turn(values, cosine, sine, orient):
    lanes = lax.broadcasted_iota(jnp.int32, values.shape, 1) % HD
    lower = pltpu.roll(values, WIDTH - ROT // 2, 1)
    upper = pltpu.roll(values, ROT // 2, 1)
    swapped = jnp.where(lanes < ROT // 2, lower, upper)
    return values * cosine + orient * swapped * sine


def wide(table):
    return jnp.concatenate([table, table], axis=1)


def row_start(lengths_ref, m, first, rows=Q_BLOCK):
    queries = first + lax.broadcasted_iota(jnp.int32, (rows, 1), 0)
    start = jnp.zeros((rows, 1), jnp.int32)
    end = jnp.int32(0)
    for doc in range(8):
        end = end + lengths_ref[m, doc]
        start = jnp.where(queries >= end, end, start)
    return queries, start


def allowed_block(lengths_ref, m, first, keys):
    queries, start = row_start(lengths_ref, m, first)
    places = lax.broadcasted_iota(jnp.int32, (Q_BLOCK, keys), 1)
    return (places >= start) & (places <= queries)


def head_mask(h):
    lanes = lax.broadcasted_iota(jnp.int32, (1, WIDTH), 1)
    return (lanes // HD == h).astype(jnp.bfloat16)


def advance(steps):
    next(steps, None)


def attention_forward(all_one, col_qkv, bias, frequency, lengths, cot):
    row_len = all_one.shape[1]
    blocks = row_len // Q_BLOCK

    def body(
        len_ref, x_in, w_ref, bias_ref, freq_ref, cot_ref,
        q_out, k_out, v_out, att_out, lse_out, cos_ref, sin_ref, cot_out, sends, recvs,
        x_ref, load_sems,
    ):
        place = Place()
        loads = [pltpu.make_async_copy(x_in.at[m], x_ref.at[m], load_sems.at[m]) for m in range(MB)]
        for load in loads:
            load.start()
        greet([place.px, place.py, place.ps])
        steps = Gather(place, cot_ref, cot_out, sends, recvs).steps()
        advance(steps)
        lanes = lax.broadcasted_iota(jnp.int32, (Q_BLOCK, 128), 1)
        for m in range(MB):
            loads[m].wait()

            def project(i, _):
                first = pl.multiple_of(i * PROJECTED, PROJECTED)
                rows = pl.ds(first, PROJECTED)
                mixed = dot(x_ref[m, rows, :], w_ref[...]) + bias_ref[...]
                places, start = row_start(len_ref, m, first, PROJECTED)
                angles = (places - start).astype(jnp.float32) * freq_ref[...]
                cosine, sine = jnp.cos(angles), jnp.sin(angles)
                cos_ref[m, rows, :] = cosine
                sin_ref[m, rows, :] = sine
                cos_wide, sin_wide = wide(cosine), wide(sine)
                q_out[m, rows, :] = turn(mixed[:, :WIDTH], cos_wide, sin_wide, 1.0).astype(
                    jnp.bfloat16
                )
                k_out[m, rows, :] = turn(
                    mixed[:, WIDTH : 2 * WIDTH], cos_wide, sin_wide, 1.0
                ).astype(jnp.bfloat16)
                v_out[m, rows, :] = mixed[:, 2 * WIDTH :].astype(jnp.bfloat16)
                return 0

            lax.fori_loop(0, row_len // PROJECTED, project, 0)
            for i in range(blocks):
                first, keys = i * Q_BLOCK, (i + 1) * Q_BLOCK
                allowed = allowed_block(len_ref, m, first, keys)
                queries = q_out[m, first:keys, :]

                def head(h, carry):
                    summed, totals_all = carry
                    mask = head_mask(h)
                    scores = dot_last(queries * mask, k_out[m, :keys, :]) * SCALE
                    scores = jnp.where(allowed, scores, MASKED)
                    peak = jnp.max(scores, axis=-1, keepdims=True)
                    raised = jnp.exp(scores - peak)
                    totals = jnp.sum(raised, axis=-1, keepdims=True)
                    probs = (raised * (1.0 / totals)).astype(jnp.bfloat16)
                    by_head = dot(probs, v_out[m, :keys, :])
                    summed = summed + by_head * mask.astype(jnp.float32)
                    totals_all = jnp.where(lanes == h, peak + jnp.log(totals), totals_all)
                    return summed, totals_all

                summed, totals_all = lax.fori_loop(
                    0,
                    WIDTH // HD,
                    head,
                    (
                        jnp.zeros((Q_BLOCK, WIDTH), jnp.float32),
                        jnp.zeros((Q_BLOCK, 128), jnp.float32),
                    ),
                    unroll=2,
                )
                att_out[m, first:keys, :] = summed.astype(jnp.bfloat16)
                lse_out[m, first:keys, :] = totals_all
                if i % 2 == 1:
                    advance(steps)
        for _ in steps:
            pass

    return kernel_call(
        body,
        [shape((MB, row_len, WIDTH))] * 4
        + [shape((MB, row_len, 128), jnp.float32)] * 3
        + [shape(WHOLE + (D,))],
        [VMEM_SPEC] * 7 + [ANY_SPEC],
        [pl.BlockSpec(memory_space=pltpu.SMEM), ANY_SPEC] + [VMEM_SPEC] * 3 + [ANY_SPEC],
        [
            DMA((GATHER_SEMS,)),
            DMA((GATHER_SEMS,)),
            pltpu.VMEM(all_one.shape, jnp.bfloat16),
            DMA((MB,)),
        ],
        4,
        (lengths, all_one, col_qkv, bias, frequency, cot),
    )


def attention_backward(
    all_branch, row_out, queries, keys, values, lse, cosine, sine, lengths, parts, residual
):
    row_len = all_branch.shape[1]
    blocks = row_len // Q_BLOCK
    def body(
        len_ref, x_in, w_ref, q_ref, k_ref, v_ref, lse_ref, cos_ref, sin_ref, parts_ref,
        res_in, mixed_out, sums_out, own, grad_k, grad_v, grad_atts, x_ref, res_ref, load_sems,
        *scratch,
    ):
        place = Place()
        pairs = [(x_in.at[m], x_ref.at[m]) for m in range(MB)] + [(res_in, res_ref)]
        loads = [
            pltpu.make_async_copy(src, dst, load_sems.at[i]) for i, (src, dst) in enumerate(pairs)
        ]
        for load in loads:
            load.start()
        greet([place.px, place.py, place.ps])

        def store(m, total):
            own[m] = (res_ref[m] + total).astype(jnp.bfloat16)

        steps = sum_steps(place, parts_ref, store, scratch)
        advance(steps)
        lanes = lax.broadcasted_iota(jnp.int32, (Q_BLOCK, 128), 1)
        for m in range(MB):
            grad_k[...] = jnp.zeros_like(grad_k)
            grad_v[...] = jnp.zeros_like(grad_v)
            loads[m].wait()
            if m == 1:
                loads[2].wait()
            grad_atts[...] = dot_last(x_ref[m], w_ref[...]).astype(jnp.bfloat16)
            q_sum = jnp.zeros((1, WIDTH), jnp.float32)
            for i in range(blocks):
                first, count = i * Q_BLOCK, (i + 1) * Q_BLOCK
                allowed = allowed_block(len_ref, m, first, count)
                query_blk = q_ref[m, first:count, :]
                grad_att = grad_atts[first:count, :]
                totals_all = lse_ref[m, first:count, :]

                def head(h, grad_q):
                    mask = head_mask(h)
                    query_h, grad_h = query_blk * mask, grad_att * mask
                    totals = jnp.sum(
                        jnp.where(lanes == h, totals_all, 0.0), axis=-1, keepdims=True
                    )
                    scores = dot_last(query_h, k_ref[m, :count, :]) * SCALE
                    probs = jnp.where(allowed, jnp.exp(scores - totals), 0.0)
                    grad_probs = dot_last(grad_h, v_ref[m, :count, :])
                    inner = jnp.sum(probs * grad_probs, axis=-1, keepdims=True)
                    grad_scores = (probs * (grad_probs - inner)).astype(jnp.bfloat16)
                    grad_k[:count, :] += dot_first(grad_scores, query_h)
                    grad_v[:count, :] += dot_first(probs.astype(jnp.bfloat16), grad_h)
                    by_head = dot(grad_scores, k_ref[m, :count, :])
                    return grad_q + by_head * mask.astype(jnp.float32)

                grad_q = lax.fori_loop(
                    0, WIDTH // HD, head, jnp.zeros((Q_BLOCK, WIDTH), jnp.float32), unroll=2
                )
                cos_wide = wide(cos_ref[m, first:count, :])
                sin_wide = wide(sin_ref[m, first:count, :])
                grad_q = (grad_q * SCALE).astype(jnp.bfloat16).astype(jnp.float32)
                grad_q = turn(grad_q, cos_wide, sin_wide, -1.0).astype(jnp.bfloat16)
                mixed_out[m, first:count, :WIDTH] = grad_q
                q_sum = q_sum + jnp.sum(grad_q.astype(jnp.float32), axis=0, keepdims=True)
                if (m, i) in ((0, 0), (0, 2), (1, 3)):
                    advance(steps)
            k_sum = jnp.zeros((1, WIDTH), jnp.float32)
            v_sum = jnp.zeros((1, WIDTH), jnp.float32)
            for i in range(blocks):
                rows = slice(i * Q_BLOCK, (i + 1) * Q_BLOCK)
                cos_wide, sin_wide = wide(cos_ref[m, rows, :]), wide(sin_ref[m, rows, :])
                part = (grad_k[rows, :] * SCALE).astype(jnp.bfloat16).astype(jnp.float32)
                part = turn(part, cos_wide, sin_wide, -1.0).astype(jnp.bfloat16)
                mixed_out[m, rows, WIDTH : 2 * WIDTH] = part
                k_sum = k_sum + jnp.sum(part.astype(jnp.float32), axis=0, keepdims=True)
                part = grad_v[rows, :].astype(jnp.bfloat16)
                mixed_out[m, rows, 2 * WIDTH :] = part
                v_sum = v_sum + jnp.sum(part.astype(jnp.float32), axis=0, keepdims=True)
            sums_out[m] = jnp.concatenate([q_sum, k_sum, v_sum], axis=1)
        for _ in steps:
            pass

    return kernel_call(
        body,
        [
            shape((MB, row_len, 3 * WIDTH)),
            shape((MB, 1, 3 * WIDTH), jnp.float32),
            shape((MB, TOK, D)),
        ],
        [VMEM_SPEC] * 3,
        [pl.BlockSpec(memory_space=pltpu.SMEM), ANY_SPEC] + [VMEM_SPEC] * 7 + [ANY_SPEC] * 2,
        [
            pltpu.VMEM((row_len, WIDTH), jnp.float32),
            pltpu.VMEM((row_len, WIDTH), jnp.float32),
            pltpu.VMEM((row_len, WIDTH), jnp.bfloat16),
            pltpu.VMEM(all_branch.shape, jnp.bfloat16),
            pltpu.VMEM(residual.shape, jnp.float32),
            DMA((MB + 1,)),
        ]
        + STEP_SCRATCH,
        7,
        (
            lengths, all_branch, row_out, queries, keys, values, lse, cosine, sine, parts, residual,
        ),
    )


def sigmoid(values):
    return 1.0 / (1.0 + jnp.exp(-values))


def tail_parts(tail):
    lower = lax.broadcasted_iota(jnp.int32, tail.shape, 1) < 64
    rolled = pltpu.roll(tail, 64, 1)
    return lower, jnp.where(lower, tail, rolled), jnp.where(lower, rolled, tail)


def feed_forward(acts, col_gu):
    def body(x_ref, w_ref, gu_out, hidden_out):
        mixed = dot(x_ref[...], w_ref[...])
        gu_out[...] = mixed
        gate, up = mixed[:, :FF_MAIN], mixed[:, FF_MAIN : 2 * FF_MAIN]
        hidden_out[:, :FF_MAIN] = (gate * sigmoid(gate) * up).astype(jnp.bfloat16)
        _, gate, up = tail_parts(mixed[:, 2 * FF_MAIN :])
        tail = (gate * sigmoid(gate) * up).astype(jnp.bfloat16)
        hidden_out[:, FF_MAIN:] = tail[:, : FF_HERE - FF_MAIN]

    count = acts.shape[0]
    rows = 512
    return pl.pallas_call(
        body,
        out_shape=[shape((count, 2 * FF_HERE), jnp.float32), shape((count, FF_HERE))],
        grid=(count // rows,),
        in_specs=[
            pl.BlockSpec((rows, D), lambda i: (i, 0)),
            pl.BlockSpec((D, 2 * FF_HERE), lambda i: (0, 0)),
        ],
        out_specs=[
            pl.BlockSpec((rows, 2 * FF_HERE), lambda i: (i, 0)),
            pl.BlockSpec((rows, FF_HERE), lambda i: (i, 0)),
        ],
        cost_estimate=pl.CostEstimate(
            flops=4 * count * D * FF_HERE, bytes_accessed=30_000_000, transcendentals=0
        ),
        compiler_params=pltpu.CompilerParams(vmem_limit_bytes=VMEM_BYTES),
    )(acts, col_gu)


def feed_backward(cots, row_down, mixed):
    def body(cot_ref, w_ref, gu_ref, grad_out):
        grad = dot_last(cot_ref[...], w_ref[...])
        main = grad[:, :FF_MAIN]
        gate, up = gu_ref[:, :FF_MAIN], gu_ref[:, FF_MAIN : 2 * FF_MAIN]
        share = sigmoid(gate)
        silu = gate * share
        grad_out[:, :FF_MAIN] = (main * up * share * (1.0 + gate * (1.0 - share))).astype(
            jnp.bfloat16
        )
        grad_out[:, FF_MAIN : 2 * FF_MAIN] = (main * silu).astype(jnp.bfloat16)
        lower, gate, up = tail_parts(gu_ref[:, 2 * FF_MAIN :])
        tail = grad[:, FF_MAIN:]
        tail = jnp.concatenate([tail, tail], axis=1)
        share = sigmoid(gate)
        by_gate = tail * up * share * (1.0 + gate * (1.0 - share))
        by_up = tail * gate * share
        grad_out[:, 2 * FF_MAIN :] = jnp.where(lower, by_gate, by_up).astype(jnp.bfloat16)

    count = cots.shape[0]
    rows = 512
    return pl.pallas_call(
        body,
        out_shape=shape((count, 2 * FF_HERE)),
        grid=(count // rows,),
        in_specs=[
            pl.BlockSpec((rows, D), lambda i: (i, 0)),
            pl.BlockSpec((FF_HERE, D), lambda i: (0, 0)),
            pl.BlockSpec((rows, 2 * FF_HERE), lambda i: (i, 0)),
        ],
        out_specs=pl.BlockSpec((rows, 2 * FF_HERE), lambda i: (i, 0)),
        cost_estimate=pl.CostEstimate(
            flops=2 * count * D * FF_HERE, bytes_accessed=30_000_000, transcendentals=0
        ),
        compiler_params=pltpu.CompilerParams(vmem_limit_bytes=VMEM_BYTES),
    )(cots, row_down, mixed)


def local_fast(
    tokens,
    doc_lengths,
    ln1_gain,
    ln1_bias,
    w_qkv,
    q_bias,
    k_bias_rot,
    v_bias,
    w_out,
    ln2_gain,
    ln2_bias,
    w_gate,
    w_up,
    w_down,
    cotangent,
):
    plane = 8
    count = Z * plane
    z_at, x_at, y_at, c_at = (lax.axis_index(name) for name in ALL)
    rank = (x_at * 2 + y_at) * 2 + c_at
    row_len = N_TOK * TOK
    block = D // count
    rot_block = HEADS * ROT // count
    ff_block = FF // count
    heads_here = HEADS // plane
    ff_here = Z * ff_block
    every = MB * row_len

    tie = lax.optimization_barrier

    pieces = [ln1_gain, ln1_bias, q_bias, v_bias, ln2_gain, ln2_bias, k_bias_rot]
    pieces = [piece.reshape(1, -1) for piece in pieces]
    here_qkv, tok_here, vectors, bias_here, lengths = prologue(
        w_qkv, tokens[:, 0], pieces, doc_lengths[:, 0]
    )

    def over_z(array):
        return lax.all_gather(array, "z", axis=0, tiled=True)

    def sum_z(term):
        return lax.psum_scatter(term, "z", scatter_dimension=0, tiled=True)

    row_out = over_z(w_out)
    here_qkv, row_out = tie((here_qkv, row_out))
    col_qkv = over_z(here_qkv.reshape(plane * block, 3 * WIDTH))
    all_one, here_gu, cot_here = first_gather(tok_here, vectors, w_gate, w_up, cotangent[:, 0])
    here_gu, w_down = tie((here_gu, w_down))
    col_gu = over_z(here_gu.reshape(plane * block, 2 * ff_here))
    row_down = over_z(w_down)

    lane = jnp.arange(128, dtype=jnp.int32) % HD
    frequency = THETA ** (-2.0 * (lane % (ROT // 2)).astype(jnp.float32) / ROT)
    frequency = jnp.where(lane < ROT // 2, -frequency, jnp.where(lane < ROT, frequency, 0.0))

    queries, keys, values, attended, lse, cos_tab, sin_tab, all_cot = attention_forward(
        all_one.reshape(MB, row_len, D),
        col_qkv,
        bias_here,
        frequency.reshape(1, 128),
        lengths,
        cot_here,
    )
    residual, all_two = out_projection(
        attended.reshape(WHOLE + (WIDTH,)), row_out, tok_here, vectors
    )
    flat_one = all_one.reshape(every, D)
    flat_two = all_two.reshape(every, D)
    flat_cot = all_cot.reshape(every, D)

    def low(term):
        return term.astype(jnp.bfloat16)

    mixed_ff, hidden = feed_forward(flat_two, col_gu)
    term_down = low(dot_first(hidden, flat_cot))
    term_down, mixed_ff = tie((term_down, mixed_ff))
    share_down = sum_z(term_down)
    grad_gu = feed_backward(flat_cot, row_down, mixed_ff)
    term_gu = low(dot_first(flat_two, grad_gu))
    term_gu, grad_gu = tie((term_gu, grad_gu))
    share_gu = sum_z(term_gu).reshape(plane, block, 2 * ff_here)
    grad_residual, all_branch, sums_two, parts = ffn_backward(
        grad_gu.reshape(WHOLE + (2 * ff_here,)), col_gu, residual, cot_here, vectors,
        hidden.reshape(WHOLE + (ff_here,)), row_down,
    )
    term_out = low(dot_first(attended.reshape(every, WIDTH), all_branch.reshape(every, D)))
    term_out, all_branch, share_down = tie((term_out, all_branch, share_down))
    share_out = sum_z(term_out)
    grad_mixed, mixed_sums, output = attention_backward(
        all_branch.reshape(MB, row_len, D),
        row_out,
        queries,
        keys,
        values,
        lse,
        cos_tab,
        sin_tab,
        lengths,
        parts,
        residual,
    )
    term_qkv = low(dot_first(flat_one, grad_mixed.reshape(every, 3 * WIDTH)))
    term_qkv, grad_mixed, share_gu = tie((term_qkv, grad_mixed, share_gu))
    share_qkv = sum_z(term_qkv)
    grad_tokens, packed, output, share_gate, share_up = input_grad(
        grad_mixed.reshape(WHOLE + (3 * WIDTH,)),
        col_qkv,
        tok_here,
        grad_residual,
        vectors,
        output,
        share_gu,
        sums_two,
        mixed_sums,
    )
    share_down, share_out = share_down.astype(jnp.float32), share_out.astype(jnp.float32)
    share_gate, share_up = share_gate.astype(jnp.float32), share_up.astype(jnp.float32)
    packed, share_down, share_out, share_gate, share_up = tie(
        (packed, share_down, share_out, share_gate, share_up)
    )
    share_qkv, grad_tokens, shares = epilogue(
        share_qkv.reshape(plane, block, 3 * WIDTH), grad_tokens, packed
    )
    small_shares = [shares[i, :block] for i in (0, 1, 2, 3, 4, 5)]
    share_k = shares[6, :rot_block]
    return (
        output[:, None],
        grad_tokens[:, None],
        small_shares[0],
        small_shares[1],
        share_qkv,
        small_shares[2],
        share_k,
        small_shares[3],
        share_out,
        small_shares[4],
        small_shares[5],
        share_gate,
        share_up,
        share_down,
    )


def solution(mesh):
    xs = mesh.shape["seq"] // Z
    ys = mesh.shape["rows"] // 2
    fine = Mesh(mesh.devices.reshape(Z, xs, ys, 2), ALL)
    acts = P(None, ("y", "core"), ("z", "x"), None)
    vec = P(ALL)
    mat = P(ALL, None)
    small_plane = xs == 2 and ys == 2
    return jax.shard_map(
        local_fast if small_plane else local,
        mesh=fine,
        in_specs=(
            acts,
            P(None, ("y", "core"), None),
            vec,
            vec,
            mat,
            vec,
            vec,
            vec,
            mat,
            vec,
            vec,
            mat,
            mat,
            mat,
            acts,
        ),
        out_specs=(acts, acts, vec, vec, mat, vec, vec, vec, mat, vec, vec, mat, mat, mat),
        check_vma=False,
    )
```

time: 3380 us -> 639 us (0.19)
  waiting for transfers between devices: 2560 us -> 9.61 us
  Pallas kernels: 0 us -> 545 us
  matrix products: 371 us -> 48.3 us
  other arithmetic: 162 us -> 8.27 us
  local copies, waits for them, and re-layouts: 115 us -> 8.57 us
  blocking collectives: 92.1 us -> 0 us
  starting transfers between devices: 44.1 us -> 0.32 us
    reduce_scatter x2 -> x4, waiting for transfers between devices: 2020 us -> 0.35 us  [sum_z(): return lax.psum_scatter(term, 'z', scatter_dimension=0, tiled=True)]
    pallas_call x0 -> x10, Pallas kernels: none -> 545 us  [the longest x8 511 us: kernel_call(): pl.pallas_call(body, out_shape=out_shape, in_specs=in_specs, out_specs=ou...]
    all_gather x5 -> x4, waiting for transfers between devices: 400 us -> 7.96 us  [over_z(): return lax.all_gather(array, 'z', axis=0, tiled=True)]
    dot_general x48 -> x0, matrix products: 283 us -> none  [the longest x10 125 us: dot_last(): lax.dot_general(left, right, (((1,), (1,)), ((), ())), preferred_element_...]
    all_to_all x8 -> x0, waiting for transfers between devices: 142 us -> none  [the longest x2 81.6 us: local(): lax.all_to_all(stacked, 'seq', split_axis=2, concat_axis=0, tiled=True)]
    concatenate x10 -> x0, other arithmetic: 110 us -> none  [the longest x1 103 us: weight_terms(): jnp.concatenate([dot_first(normed_one, grad_mixed), dot_first(attended, g...]
    unnamed x2 -> x0, blocking collectives: 92.1 us -> none
    all_to_all x8 -> x0, starting transfers between devices: 43.4 us -> none  [the longest x2 15.2 us: local(): lax.all_to_all(attended_heads, 'seq', split_axis=0, concat_axis=1, tiled=...]
  transfers between devices with their start and end apart: 15 -> 8, of which waited for: 12 -> 2; matrix products, arithmetic and copies ran while one was open for 11% -> 9% of each run, Pallas kernels for 0% -> 79%
where the time goes in v1:
time: 639 us; the launch traced here: 635 us
  Pallas kernels  545 us (85%)
  matrix products  48.3 us (8%)
  between operations  14.6 us (2%)
  waiting for transfers between devices  9.61 us (2%)
  local copies, waits for them, and re-layouts  8.57 us (1%)
  other arithmetic  8.27 us (1%)
    pallas_call x8, Pallas kernels, kernel_call(): pl.pallas_call(body, out_shape=out_shape, in_specs=in_specs, out_specs=ou...  511 us
    dot_general x4, matrix products, dot_first(): lax.dot_general(left, right, (((0,), (0,)), ((), ())), preferred_element_...  48.3 us
    pallas_call x1, Pallas kernels, feed_forward(): pl.pallas_call(body, out_shape=[shape((count, 2 * FF_HERE), jnp.float32),...  19.2 us
    pallas_call x1, Pallas kernels, feed_backward(): pl.pallas_call(body, out_shape=shape((count, 2 * FF_HERE)), grid=(count /...  14.5 us
  transfers between devices with their start and end apart: 8, of which 2 were waited for; matrix products, arithmetic and copies ran while one was open for 9% of the time, Pallas kernels for 79%

profile of v1, /device:TPU:1, one launch (start us, length us, event | category | flops | bytes accessed | tf_op | source)
XLA Modules:
  0.0 634.7 jit_solution(11546552193296378021)
XLA Ops:
  7.2 0.7 all-gather.5.cloned.1.call-update
  7.9 0.0 all-gather.7.cloned.1.call-start
  8.0 45.7 %shard_map.254 = (bf16[8,64,768]{2,1,0:T(8,128)(2,1)}, bf16[2,128,2048]{2,1,0:T(8,128)(2,1)}, f32[8,2048]{1,0:T(8,128)}, f32[1,768]{1,0:T(1,128)}, s32[2,8]{1,0:T(2,128)}) custom-call(bf16[64,6144]{1,0:T(8,128)(2,1)} %qkv_ref.1, bf16[2,128,2048]{2,1,0:T(8,128)(2,1)} %bitcast.69, bf16[1,64]{1,0:T(2,128)(2,1)} %bitcast.75, bf16[1,64]{1,0:T(2,128)(2,1)} %bitcast.76, ...), custom_call_target="tpu_custom_call" | custom-call | tf_op jit(solution)/shard_map/pallas_call | solution.py:844
  53.8 75.9 %shard_map.255 = (bf16[2,2,2,2,128,2048]{5,4,3,2,1,0:T(8,128)(2,1)}, bf16[8,64,1408]{2,1,0:T(8,128)(2,1)}, bf16[2,128,2048]{2,1,0:T(8,128)(2,1)}) custom-call(bf16[2,128,2048]{2,1,0:T(8,128)(2,1)} %get-tuple-element.68.tok_ref, f32[8,2048]{1,0:T(8,128)} %get-tuple-element.69.vec_ref, bf16[64,5632]{1,0:T(8,128)(2,1)} %gate_ref.1, bf16[64,5632]{1,0:T(8,128)(2,1)} %up_ref.1, ...), custom_call_target="tpu_custom_call" | custom-call | tf_op jit(solution)/shard_map/pallas_call | solution.py:844
  129.7 0.0 all-gather.9.cloned.1.call-start
  129.7 0.5 all-gather.9.cloned.1.call-update
  130.3 0.5 compare_select_fusion.3.freq_ref
  130.8 7.9 %all-gather.7.cloned.1.call-done.w_ref.weight_ref = bf16[2048,768]{1,0:T(8,128)(2,1)} async-done(((bf16[512,768]{1,0:T(8,128)(2,1)}), bf16[2048,768]{1,0:T(8,128)(2,1)}) %all-gather.7.cloned.1.call-update) | async-done | bytes 3145744 | tf_op jit(solution)/shard_map/all_gather | solution.py:1728
  138.7 51.9 %shard_map.256 = (bf16[2,1024,256]{2,1,0:T(8,128)(2,1)}, bf16[2,1024,256]{2,1,0:T(8,128)(2,1)}, bf16[2,1024,256]{2,1,0:T(8,128)(2,1)}, bf16[2,1024,256]{2,1,0:T(...) custom-call(s32[2,8]{1,0:T(2,128)} %get-tuple-element.71.len_ref, ...), custom_call_target="tpu_custom_call" | custom-call | tf_op jit(solution)/shard_map/pallas_call | solution.py:844
  190.6 84.8 %shard_map.257 = (f32[2,128,2048]{2,1,0:T(8,128)}, bf16[2,2,2,2,128,2048]{5,4,3,2,1,0:T(8,128)(2,1)}) custom-call(bf16[2,2,2,2,128,256]{5,4,3,2,1,0:T(8,128)(2,1)} %bitcast.61, bf16[256,2048]{1,0:T(8,128)(2,1)} %all-gather.5.cloned.1.call-done.weight_ref.w_ref, bf16[2,128,2048]{2,1,0:T(8,128)(2,1)} %get-tuple-element.68.tok_ref, ...), custom_call_target="tpu_custom_call" | custom-call | tf_op jit(solution)/shard_map/pallas_call | solution.py:844
  275.5 19.2 %shard_map.258 = (f32[2048,1408]{1,0:T(8,128)}, bf16[2048,704]{1,0:T(8,128)(2,1)}) custom-call(bf16[2048,2048]{1,0:T(8,128)(2,1)} %bitcast.82, bf16[2048,1408]{1,0:T(8,128)(2,1)} %all-gather.11.cloned.1.call-done.w_ref.weight_ref), custom_call_target="tpu_custom_call" | custom-call | flops 11811160064 | bytes 30000000 | tf_op jit(solution)/shard_map/pallas_call | solution.py:1633
  294.7 10.7 %convolution_convert_fusion.2 = bf16[704,2048]{1,0:T(8,128)(2,1)} fusion(bf16[2048,704]{1,0:T(8,128)(2,1)} %get-tuple-element.83, bf16[2048,2048]{1,0:T(8,128)(2,1)} %bitcast.57), kind=kOutput, calls=%fused_computation.2 | convolution fusion | flops 5907021824 | bytes 14155776 | tf_op jit(solution)/shard_map/dot_general | solution.py:32
  305.4 0.0 reduce-scatter.7.cloned.1.call-start
  305.5 14.5 %shard_map.259 = bf16[2048,1408]{1,0:T(8,128)(2,1)} custom-call(bf16[2048,2048]{1,0:T(8,128)(2,1)} %bitcast.58, bf16[704,2048]{1,0:T(8,128)(2,1)} %all-gather.9.cloned.1.call-done.w_ref.down_in, f32[2048,1408]{1,0:T(8,128)} %get-tuple-element.85.gu_ref), custom_call_target="tpu_custom_call" | custom-call | flops 5905580032 | bytes 30000000 | tf_op jit(solution)/shard_map/pallas_call | solution.py:1673
  320.0 19.1 %convolution_convert_fusion = bf16[2048,1408]{1,0:T(8,128)(2,1)} fusion(bf16[2048,2048]{1,0:T(8,128)(2,1)} %bitcast.83, bf16[2048,1408]{1,0:T(8,128)(2,1)} %shard_map.259), kind=kOutput, calls=%fused_computation | convolution fusion | flops 11814043648 | bytes 19922944 | tf_op jit(solution)/shard_map/dot_general | solution.py:32
  339.2 0.0 reduce-scatter.11.cloned.1.call-start
  339.3 86.9 %shard_map.260 = (f32[2,128,2048]{2,1,0:T(8,128)}, bf16[2,2,2,2,128,2048]{5,4,3,2,1,0:T(8,128)(2,1)}, f32[2,2048]{1,0:T(2,128)}, bf16[2,2,2,2,128,2048]{5,4,3,2,1,0:T(8,128)(2,1)}) custom-call(bf16[2,2,2,2,128,1408]{5,4,3,2,1,0:T(8,128)(2,1)} %bitcast.56, bf16[2048,1408]{1,0:T(8,128)(2,1)} %all-gather.11.cloned.1.call-done.w_ref.weight_ref, ...), custom_call_target="tpu_custom_call" | custom-call | tf_op jit(solution)/shard_map/pallas_call | solution.py:844
  426.1 6.7 %convolution_convert_fusion.3 = bf16[256,2048]{1,0:T(8,128)(2,1)} fusion(bf16[2048,256]{1,0:T(8,128)(2,1)S(1)} %bitcast.62, bf16[2048,2048]{1,0:T(8,128)(2,1)} %bitcast.54), kind=kOutput, calls=%fused_computation.3 | convolution fusion | flops 2148007936 | bytes 10485760 | tf_op jit(solution)/shard_map/dot_general | solution.py:32
  432.9 49.1 %shard_map.261 = (bf16[2,1024,768]{2,1,0:T(8,128)(2,1)}, f32[2,1,768]{2,1,0:T(1,128)}, bf16[2,128,2048]{2,1,0:T(8,128)(2,1)}) custom-call(s32[2,8]{1,0:T(2,128)} %get-tuple-element.71.len_ref, bf16[2,1024,2048]{2,1,0:T(8,128)(2,1)} %bitcast.55, bf16[256,2048]{1,0:T(8,128)(2,1)} %all-gather.5.cloned.1.call-done.weight_ref.w_ref, ...), custom_call_target="tpu_custom_call" | custom-call | tf_op jit(solution)/shard_map/pallas_call | solution.py:844
  482.0 11.7 %convolution_convert_fusion.1 = bf16[2048,768]{1,0:T(8,128)(2,1)} fusion(bf16[2048,2048]{1,0:T(8,128)(2,1)} %bitcast.60, bf16[2048,768]{1,0:T(8,128)(2,1)} %bitcast.64), kind=kOutput, calls=%fused_computation.1 | convolution fusion | flops 6444023808 | bytes 14680064 | tf_op jit(solution)/shard_map/dot_general | solution.py:32
  493.8 1.3 convert_element_type.39
  495.0 0.3 reduce-scatter.11.cloned.1.call-done
  495.4 1.8 convert_element_type.40
  497.1 73.3 %shard_map.262 = (bf16[2,128,2048]{2,1,0:T(8,128)(2,1)}, f32[8,4,8,128]{3,2,1,0:T(8,128)}, bf16[2,128,2048]{2,1,0:T(8,128)(2,1)}, bf16[64,5632]{1,0:T(8,128)(2,1)}, bf16[64,5632]{1,0:T(8,128)(2,1)}) custom-call(bf16[2,2,2,2,128,768]{5,4,3,2,1,0:T(8,128)(2,1)} %bitcast.65, bf16[2048,768]{1,0:T(8,128)(2,1)} %all-gather.7.cloned.1.call-done.w_ref.weight_ref, ...), custom_call_target="tpu_custom_call" | custom-call | tf_op jit(solution)/shard_map/pallas_call | solution.py:844
  570.4 2.4 convert_element_type.41
  572.8 2.3 convert_element_type.42
  575.2 43.9 %shard_map.263 = (f32[64,6144]{1,0:T(8,128)}, bf16[2,128,2048]{2,1,0:T(8,128)(2,1)}, f32[8,128]{1,0:T(8,128)}) custom-call(bf16[8,64,768]{2,1,0:T(8,128)(2,1)} %bitcast.73, bf16[2,128,2048]{2,1,0:T(8,128)(2,1)} %get-tuple-element.108.tok_ref, f32[8,4,8,128]{3,2,1,0:T(8,128)} %get-tuple-element.114.packed_ref), custom_call_target="tpu_custom_call" | custom-call | tf_op jit(solution)/shard_map/pallas_call | solution.py:844
  619.0 1.2 slice_bitcast_fusion.3
  620.2 1.4 slice_bitcast_fusion
  621.6 1.0 copy.34
  622.6 2.3 copy.35
  624.9 2.7 copy.36
  (22 shorter events, 0.3 us)
Async XLA Ops:
  7.2 46.5 %all-gather.5.cloned.1.call-start = ((), (), s32[]{:S(2)}) async-start(), calls=%async_computation.4 | async-start | bytes 1310720 | tf_op jit(solution)/shard_map/all_gather | solution.py:1728
  7.9 130.8 %all-gather.7.cloned.1.call-start = ((), (), s32[]{:S(2)}) async-start(), calls=%async_computation.5 | async-start | bytes 3932160 | tf_op jit(solution)/shard_map/all_gather | solution.py:1728
  53.7 221.7 %all-gather.11.cloned.1.call-start = ((), (), s32[]{:S(2)}) async-start(), calls=%async_computation.7 | async-start | bytes 7208960 | tf_op jit(solution)/shard_map/all_gather | solution.py:1728
  129.7 175.8 %all-gather.9.cloned.1.call-start = ((), (), s32[]{:S(2)}) async-start(), calls=%async_computation.6 | async-start | bytes 3604480 | tf_op jit(solution)/shard_map/all_gather | solution.py:1728
  130.2 302.6 %reduce-scatter.5.cloned.1.call-start = ((), (), s32[]{:S(2)}) async-start(), calls=%async_computation.8 | async-start | bytes 3604480 | tf_op jit(solution)/shard_map/reduce_scatter | solution.py:1731
  305.4 188.3 %reduce-scatter.7.cloned.1.call-start = ((), (), s32[]{:S(2)}) async-start(), calls=%async_computation.9 | async-start | bytes 7208960 | tf_op jit(solution)/shard_map/reduce_scatter | solution.py:1731
  339.2 156.2 %reduce-scatter.11.cloned.1.call-start = ((), (), s32[]{:S(2)}) async-start(), calls=%async_computation.11 | async-start | bytes 1310720 | tf_op jit(solution)/shard_map/reduce_scatter | solution.py:1731
  339.2 86.9 %copy-start = (bf16[2,1024,256]{2,1,0:T(8,128)(2,1)S(1)}, bf16[2,1024,256]{2,1,0:T(8,128)(2,1)}, u32[]{:S(2)}) copy-start(bf16[2,1024,256]{2,1,0:T(8,128)(2,1)} %get-tuple-element.76) | copy-start | bytes 3145732
  432.9 142.3 %reduce-scatter.9.cloned.1.call-start = ((), (), s32[]{:S(2)}) async-start(), calls=%async_computation.10 | async-start | bytes 3932160 | tf_op jit(solution)/shard_map/reduce_scatter | solution.py:1731
  482.0 11.8 %copy-start.2 = (bf16[176,2048]{1,0:T(8,128)(2,1)S(1)}, bf16[176,2048]{1,0:T(8,128)(2,1)}, u32[]{:S(2)}) copy-start(bf16[176,2048]{1,0:T(8,128)(2,1)} %reduce-scatter.5.cloned.1.call-done) | copy-start | bytes 2162692
  570.4 51.2 %copy-start.1 = (bf16[2,128,2048]{2,1,0:T(8,128)(2,1)S(1)}, bf16[2,128,2048]{2,1,0:T(8,128)(2,1)}, u32[]{:S(2)}) copy-start(bf16[2,128,2048]{2,1,0:T(8,128)(2,1)} %get-tuple-element.106) | copy-start | bytes 3145732
Sparse Core Ops, SparseCore 0:
  9.6 44.0 all-gather.4
  55.3 83.4 all-gather.6
  140.3 104.5 all-gather.10
  246.3 57.2 all-gather.8
  305.7 54.7 reduce-scatter.4
  362.6 102.3 reduce-scatter.6
  467.8 27.4 reduce-scatter.10
  497.8 75.6 reduce-scatter.8
